TPU v7x, 128 devices: a whole 4x4x4 slice. The times are simulated.
128 devices in a mesh: gx: 8 (over z, core), gy: 16 (over y, x).
Axes of the slice: x: 4, y: 4, z: 4, core: 2. Of those that a mesh axis runs over, the one named last changes fastest.
Arguments:
- ensemble: float32 [64, 256, 16384], P(None, 'gx', 'gy'), may hold values from -15 to 15
- obs_index: int32 [65536], P(('gx', 'gy')), may hold values from 0 to 1023
- obs_scale: float32 [65536], P(('gx', 'gy')), may hold values from 0.005 to 0.15
- member_order: int32 [64], replicated, may hold values from 0 to 63, each once
Outputs:
- analysis: float32 [64, 256, 16384], P(None, 'gx', 'gy')
Inputs may be any that keep to these rules, and one draw needn't show every extreme that they name: `obs_index`: entries of block d (positions d * 512 to (d + 1) * 512 - 1) are local mode numbers of that block; values may repeat. `member_order`: A permutation of 0 to 63.
All inputs are finite; a program needn't handle non-finite values.
Results may differ from a plain program's by a relative error of at most 0.0001.
Values sent between devices are 32-bit elements; how exact they have to be, the bound alone decides.
No kernel may reach another device: no remote copies, remote signals or barrier semaphores. Data moves between devices by JAX's collectives and lax.ppermute only.
A program may use at most 128 MiB of HBM per device.

v0:
```python
import math

import jax
import jax.numpy as jnp
import numpy as np
from jax import lax
from jax.experimental import pallas as pl
from jax.experimental.pallas import tpu as pltpu
from jax.sharding import PartitionSpec as P

M = 64
NX = 256
NY = 256
NZ = 64
XM = 64
YM = 64
ZM = 32
NS_ITERS = 18
OBS_DEV = 512
GX = 8
GY = 16
LX = NX // GX
LY = NY // GY

exact_mode = lax.Precision.HIGHEST
f32 = jnp.float32
bf16 = jnp.bfloat16


def basis(length, count):
    q = np.arange(length)
    r = np.arange(count)
    half = count // 2
    freq = np.where(r < half, r, r - half + 1)
    phase = (freq[:, None] * q[None, :] % length) * (2.0 * math.pi / length)
    scale = np.where(r == 0, math.sqrt(1.0 / length), math.sqrt(2.0 / length))
    return scale[:, None] * np.where((r < half)[:, None], np.cos(phase), np.sin(phase))


def two_parts(table, axis):
    high = table.astype(np.float32).astype(jnp.bfloat16)
    low = (table - high.astype(np.float64)).astype(np.float32).astype(jnp.bfloat16)
    return np.concatenate([high, low], axis=axis)


def depth_tables():
    bz = basis(NZ, ZM)
    out = np.zeros((GX, 128, 256))
    for g in range(GX):
        for y4 in range(4):
            cols = slice(64 * y4, 64 * y4 + 64)
            for h in range(GY):
                out[g, 16 * y4 + h, cols] = bz[2 * h + 1]
            for s in range(GX):
                for c2 in range(2):
                    out[g, 64 + 8 * s + 2 * y4 + c2, cols] = bz[4 * ((g + s) % GX) + 2 * c2]
    return two_parts(out, 1)


def first_tables():
    bx = basis(NX, XM)
    out = np.zeros((GX, 2, XM, GX, LX // 2))
    for g in range(GX):
        for s in range(GX):
            start = LX * ((g - s) % GX)
            block = bx[:, start : start + LX]
            out[g, 0, :, s, :] = block[:, 0::2]
            out[g, 1, :, s, :] = block[:, 1::2]
    return two_parts(out.reshape(GX, 2 * XM, GX * LX // 2), 1)


def second_tables():
    by = basis(NY, YM)
    out = np.stack(
        [np.concatenate([by[8 * ((g + s) % GX) :][:8] for s in range(GX)]) for g in range(GX)]
    )
    return two_parts(out, 1)


def split(value):
    high = value.astype(bf16)
    return high, (value - high.astype(f32)).astype(bf16)


def three_parts(value):
    high = value.astype(bf16)
    rest = value - high.astype(f32)
    middle = rest.astype(bf16)
    return high, middle, (rest - middle.astype(f32)).astype(bf16)


def contract(table, value, dims):
    rows = table.shape[0] // 2
    high, low = split(value)
    first = lax.dot_general(table, high, (dims, ((), ())), preferred_element_type=f32)
    second = lax.dot_general(table[:rows], low, (dims, ((), ())), preferred_element_type=f32)
    return first[:rows] + first[rows:] + second


NN = ((1,), (0,))
NT = ((1,), (1,))


def half_lanes(shape):
    return lax.broadcasted_iota(jnp.int32, shape, 1) < 64


def mode_weights(index, scale):
    square = scale * (1.0 / math.sqrt(M - 1))
    square = square * square
    high = lax.broadcasted_iota(jnp.int32, (16, OBS_DEV), 0) == (index >> 6)
    low = lax.broadcasted_iota(jnp.int32, (XM, OBS_DEV), 0) == (index & 63)
    parts = jnp.concatenate(
        [jnp.where(high, part.astype(f32), 0.0) for part in three_parts(square)]
    ).astype(bf16)
    sums = lax.dot_general(
        parts, low.astype(f32).astype(bf16), (NT, ((), ())), preferred_element_type=f32
    )
    return sums[:16] + sums[16:32] + sums[32:]


def depth_kernel(place, *refs):
    del place
    tiles, table_ref, index, scale = refs[:8], refs[8], refs[9], refs[10]
    cross_ref, odd_weight, row_refs = refs[11], refs[12], refs[13:]
    step = pl.program_id(0)

    @pl.when(step == 0)
    def _():
        weight = mode_weights(index[...], scale[...])
        weight = jnp.concatenate([weight, jnp.zeros((16, 64), f32)], axis=1)
        odd_weight[...] = weight[8:]
        for ref in row_refs:
            ref[512:520, :] = weight[:8]

    means = [jnp.sum(tile[...], axis=0) * (1.0 / M) for tile in tiles]
    flats = [tile.reshape(M * 8, 128) for tile in tiles]
    cross = cross_ref.reshape(GY * 4 * LY, 128)
    table = table_ref[0]
    for group in range(2):
        for quad in range(4):
            block = jnp.concatenate(
                [
                    jnp.concatenate(
                        [
                            flats[t][pl.ds(x, M, stride=8), :] - means[t][x : x + 1]
                            for t in (2 * quad, 2 * quad + 1)
                        ],
                        axis=1,
                    )
                    for x in range(4 * group, 4 * group + 4)
                ]
            )
            modes = contract(table, block, NT)
            for pair in range(2):
                lanes = slice(128 * pair, 128 * pair + 128)
                p = 2 * group + pair
                for y4 in range(4):
                    cross[pl.ds(LY * p + 4 * quad + y4, GY, stride=4 * LY), :] = modes[
                        16 * y4 : 16 * y4 + 16, lanes
                    ]
                for shift in range(GX):
                    start = pl.multiple_of(128 * step + 32 * p + 8 * quad, 8)
                    row_refs[shift][pl.ds(start, 8), :] = modes[
                        64 + 8 * shift : 72 + 8 * shift, lanes
                    ]


def depth_modes(place, ensemble, tables, index, scale):
    tile = lambda t: pl.BlockSpec((M, 8, 128), lambda i, place: (0, i, t))
    grid_spec = pltpu.PrefetchScalarGridSpec(
        num_scalar_prefetch=1,
        grid=(LX // 8,),
        in_specs=[tile(t) for t in range(8)]
        + [pl.BlockSpec((1, 256, 256), lambda i, place: (place[0], 0, 0))]
        + [pl.BlockSpec((1, OBS_DEV), lambda i, place: (0, 0))] * 2,
        out_specs=[
            pl.BlockSpec((GY, 4, LY, 128), lambda i, place: (0, i, 0, 0)),
            pl.BlockSpec((8, 128), lambda i, place: (0, 0)),
        ]
        + [pl.BlockSpec((520, 128), lambda i, place: (0, 0))] * GX,
    )
    return pl.pallas_call(
        depth_kernel,
        grid_spec=grid_spec,
        out_shape=[pltpu.HBM((GY, LX // 2, LY, 128), f32), pltpu.HBM((8, 128), f32)]
        + [pltpu.HBM((520, 128), f32)] * GX,
        compiler_params=pltpu.CompilerParams(vmem_limit_bytes=48 << 20),
        name="depth_modes",
    )(place, *[ensemble] * 8, tables, index, scale)


def first_kernel(place, table_ref, *refs):
    blocks, out_ref, held = refs[:GX], refs[GX], refs[GX + 1]
    out = out_ref.reshape(XM * 18, 128)
    held[64:, :] = jnp.zeros((64, 128), f32)
    for shift in range(GX):
        start = pl.multiple_of(8 * ((place[0] + GX - shift) % GX), 8)
        held[pl.ds(start, 8), :] = blocks[shift][512:520, :]
    out[pl.ds(16, XM, stride=18), :] = held[...].T[:64]
    out[pl.ds(17, XM, stride=18), :] = jnp.zeros((XM, 128), f32)
    table = table_ref[0]
    left = half_lanes((XM, 128))
    for y in range(LY):
        value = jnp.concatenate(
            [
                jnp.concatenate([b[pl.ds(2 * y + c2, 16, stride=32), :] for b in blocks])
                for c2 in range(2)
            ],
            axis=1,
        )
        both = contract(table, value, NN)
        even, odd = both[:, :128], both[:, 128:]
        out[pl.ds(y, XM, stride=18), :] = jnp.where(
            left,
            even[:XM] + pltpu.roll(even[XM:], 64, 1),
            pltpu.roll(odd[:XM], 64, 1) + odd[XM:],
        )


def first_modes(place, tables, blocks):
    grid_spec = pltpu.PrefetchScalarGridSpec(
        num_scalar_prefetch=1,
        grid=(1,),
        in_specs=[pl.BlockSpec((1, 256, 128), lambda i, place: (place[0], 0, 0))]
        + [pl.BlockSpec((520, 128), lambda i, place: (0, 0))] * GX,
        out_specs=pl.BlockSpec((GY, 72, 128), lambda i, place: (0, 0, 0)),
        scratch_shapes=[pltpu.VMEM((128, 128), f32)],
    )
    return pl.pallas_call(
        first_kernel,
        grid_spec=grid_spec,
        out_shape=pltpu.HBM((GY, 72, 128), f32),
        compiler_params=pltpu.CompilerParams(vmem_limit_bytes=32 << 20),
        name="first_modes",
    )(place, tables, *blocks)


def second_kernel(place, table_ref, cross, *outs):
    del place
    step = pl.program_id(0)
    table = table_ref[0]
    for half in range(2):
        value = jnp.concatenate(
            [
                jnp.concatenate([cross[h, 2 * half + pair] for h in range(GY)])
                for pair in range(2)
            ],
            axis=1,
        )
        modes = contract(table, value, NN)
        for pair in range(2):
            for shift in range(GX):
                outs[shift].reshape(128, 128)[
                    pl.ds(4 * step + 2 * half + pair, 8, stride=16), :
                ] = modes[8 * shift : 8 * shift + 8, 128 * pair : 128 * pair + 128]


def second_modes(place, tables, cross):
    grid_spec = pltpu.PrefetchScalarGridSpec(
        num_scalar_prefetch=1,
        grid=(4,),
        in_specs=[
            pl.BlockSpec((1, 128, 256), lambda i, place: (place[0], 0, 0)),
            pl.BlockSpec((GY, 4, LY, 128), lambda i, place: (0, i, 0, 0)),
        ],
        out_specs=[pl.BlockSpec((8, 16, 128), lambda i, place: (0, 0, 0))] * GX,
    )
    return pl.pallas_call(
        second_kernel,
        grid_spec=grid_spec,
        out_shape=[pltpu.HBM((8, 16, 128), f32)] * GX,
        compiler_params=pltpu.CompilerParams(vmem_limit_bytes=32 << 20),
        name="second_modes",
    )(place, tables, cross)


def gram_kernel(place, first_table, second_table, odd_weight, even_ref, *refs):
    odd_refs, out = refs[:GX], refs[GX]
    left = half_lanes((64, 128))
    total = jnp.zeros((128, 128), f32)

    def add(rows, one, two):
        top = lax.broadcasted_iota(jnp.int32, (128, 256), 0) < 64
        weight = jnp.where(top, jnp.concatenate(one, axis=1), jnp.concatenate(two, axis=1))
        return jnp.dot(
            rows.T * weight, rows, precision=exact_mode, preferred_element_type=f32
        )

    table = second_table[...]
    rows = []
    for pair in range(2):
        value = jnp.concatenate(
            [
                jnp.concatenate([even_ref[h, 18 * a : 18 * a + 16] for h in range(GY)])
                for a in (2 * pair, 2 * pair + 1)
            ],
            axis=1,
        )
        modes = contract(table, value, NN)
        rows += [modes[:, :128], modes[:, 128:]]
    weights = [
        [even_ref[2 * place[0] + c2, 18 * a + 16 : 18 * a + 17, :64] for a in range(4)]
        for c2 in range(2)
    ]
    total += add(jnp.concatenate(rows), *weights)
    table = first_table[0]
    rows = []
    for pair in range(4):
        value = jnp.concatenate(
            [
                jnp.concatenate([ref[b] for ref in odd_refs])
                for b in (2 * pair, 2 * pair + 1)
            ],
            axis=1,
        )
        both = contract(table, value, NN)
        one, two = both[:, :128], both[:, 128:]
        rows.append(
            jnp.where(
                left,
                one[:XM] + pltpu.roll(one[XM:], 64, 1),
                pltpu.roll(two[:XM], 64, 1) + two[XM:],
            )
        )
    weights = [[odd_weight[b : b + 1, :64] for b in range(b2, 8, 2)] for b2 in range(2)]
    total += add(jnp.concatenate(rows), *weights)
    gram = total[:64] + pltpu.roll(total[64:], 64, 1)
    packed = jnp.where(half_lanes((32, 128)), gram[:32], pltpu.roll(gram[32:], 64, 1))
    for i in range(GY):
        out[i] = packed


def gram(place, first_table, second_table, odd_weight, even, odd):
    whole = lambda *shape: pl.BlockSpec(shape, lambda i, place: (0,) * len(shape))
    grid_spec = pltpu.PrefetchScalarGridSpec(
        num_scalar_prefetch=1,
        grid=(1,),
        in_specs=[
            pl.BlockSpec((1, 256, 128), lambda i, place: (place[0], 0, 0)),
            whole(128, 256),
            whole(8, 128),
            whole(GY, 72, 128),
        ]
        + [whole(8, 16, 128)] * GX,
        out_specs=whole(GY, 32, 128),
    )
    return pl.pallas_call(
        gram_kernel,
        grid_spec=grid_spec,
        out_shape=pltpu.HBM((GY, 32, 128), f32),
        compiler_params=pltpu.CompilerParams(vmem_limit_bytes=32 << 20),
        name="gram",
    )(place, first_table, second_table, odd_weight, even, *odd)


def add_kernel(parts, out):
    total = jnp.sum(parts[...], axis=0)
    for i in range(GX):
        out[i] = total


def add_parts(parts):
    return pl.pallas_call(
        add_kernel, out_shape=pltpu.HBM((GX, 32, 128), f32), name="add_parts"
    )(parts)


def exact_dot(one, two):
    a, b, c = three_parts(one)
    d, e, f = three_parts(two)
    first = jnp.dot(
        jnp.concatenate([a, a, b, a], axis=1),
        jnp.concatenate([d, e, d, f]),
        preferred_element_type=f32,
    )
    second = jnp.dot(
        jnp.concatenate([b, c], axis=1), jnp.concatenate([e, d]), preferred_element_type=f32
    )
    return first + second


def combine_table(parts, order):
    packed = jnp.sum(parts, axis=0)
    row = lax.broadcasted_iota(jnp.int32, (M, M), 0)
    column = lax.broadcasted_iota(jnp.int32, (M, M), 1)
    identity = (row == column).astype(f32)
    matrix = identity + jnp.concatenate([packed[:, :64], packed[:, 64:]])
    squares = jnp.sum(jnp.sum(matrix * matrix, axis=1, keepdims=True), axis=0, keepdims=True)
    frobenius = jnp.sqrt(squares)

    def sweep(turn, carry):
        root, inverse = carry
        change = 1.5 * identity - 0.5 * exact_dot(inverse, root)
        return exact_dot(root, change), exact_dot(change, inverse)

    _, inverse = lax.fori_loop(0, NS_ITERS, sweep, (matrix / frobenius, identity))
    transform = inverse / jnp.sqrt(frobenius)
    chosen = (order == column).astype(f32)
    weight = lax.dot_general(
        chosen, transform, (NT, ((), ())), precision=exact_mode, preferred_element_type=f32
    )
    high, low = split(weight)
    high, low = high.astype(f32), low.astype(f32)
    none = jnp.zeros((M, M), f32)
    return jnp.concatenate(
        [
            jnp.concatenate([high, high, none, none], axis=1),
            jnp.concatenate([low, none, none, none], axis=1),
            jnp.concatenate([none, none, high, high], axis=1),
            jnp.concatenate([none, none, low, none], axis=1),
        ]
    ).astype(bf16)


def analysis_kernel(parts, order, ens_hbm, out_hbm, ens, out, weights, fetched, stored):
    def fetch(n):
        i, t = n // 8, n % 8
        place = (slice(None), pl.ds(8 * i, 8), pl.ds(128 * t, 128))
        return pltpu.make_async_copy(ens_hbm.at[place], ens.at[n], fetched.at[n])

    def store(n):
        i, t = n // 8, n % 8
        place = (slice(None), pl.ds(8 * i, 8), pl.ds(128 * t, 128))
        return pltpu.make_async_copy(out.at[n], out_hbm.at[place], stored.at[n])

    count = LX * LY * NZ // 1024
    for n in range(count):
        fetch(n).start()
    weights[...] = combine_table(parts[...], order[...])

    @pl.loop(0, count // 2)
    def _(turn):
        table = weights[...]
        tiles = (2 * turn, 2 * turn + 1)
        for n in tiles:
            fetch(n).wait()
        means = [jnp.sum(ens[n], axis=0) * (1.0 / M) for n in tiles]
        flats = [ens.at[n].reshape(M * 8, 128) for n in tiles]
        outs = [out.at[n].reshape(M * 8, 128) for n in tiles]
        for x in range(0, 8, 2):
            value = []
            for i in (x, x + 1):
                value += split(
                    jnp.concatenate(
                        [flats[k][pl.ds(i, M, stride=8), :] - means[k][i : i + 1] for k in range(2)],
                        axis=1,
                    )
                )
            result = jnp.dot(table, jnp.concatenate(value), preferred_element_type=f32)
            for i in range(2):
                sums = result[128 * i : 128 * i + 64] + result[128 * i + 64 : 128 * i + 128]
                for k in range(2):
                    outs[k][pl.ds(x + i, M, stride=8), :] = sums[:, 128 * k : 128 * k + 128]
        for n in tiles:
            store(n).start()

    for n in range(count):
        store(n).wait()


def analyse(parts, order, ensemble):
    count = LX * LY * NZ // 1024
    return pl.pallas_call(
        analysis_kernel,
        in_specs=[
            pl.BlockSpec(memory_space=pltpu.VMEM),
            pl.BlockSpec(memory_space=pltpu.VMEM),
            pl.BlockSpec(memory_space=pl.ANY),
        ],
        out_specs=pl.BlockSpec(memory_space=pl.ANY),
        out_shape=jax.ShapeDtypeStruct((M, LX, LY * NZ), f32),
        scratch_shapes=[
            pltpu.VMEM((count, M, 8, 128), f32),
            pltpu.VMEM((count, M, 8, 128), f32),
            pltpu.VMEM((256, 256), bf16),
            pltpu.SemaphoreType.DMA((count,)),
            pltpu.SemaphoreType.DMA((count,)),
        ],
        compiler_params=pltpu.CompilerParams(vmem_limit_bytes=40 << 20),
        name="analysis",
    )(parts, order, ensemble)


def shifted(block, shift):
    return lax.ppermute(block, "gx", [(i, (i + shift) % GX) for i in range(GX)])


def on_device(ensemble, obs_index, obs_scale, member_order):
    gx = lax.axis_index("gx")
    place = gx.astype(jnp.int32).reshape(1)
    ensemble = pltpu.with_memory_space_constraint(ensemble, pltpu.HBM)
    first_table = jnp.asarray(first_tables())
    cross, odd_weight, *rows = depth_modes(
        place,
        ensemble,
        jnp.asarray(depth_tables()),
        obs_index.reshape(1, OBS_DEV),
        obs_scale.reshape(1, OBS_DEV),
    )
    cross = lax.all_to_all(cross, "gy", split_axis=0, concat_axis=0, tiled=True)
    rows = [rows[0]] + [shifted(rows[s], s) for s in range(1, GX)]

    even = first_modes(place, first_table, rows)
    even = lax.all_to_all(even, "gy", split_axis=0, concat_axis=0, tiled=True)
    odd = second_modes(place, jnp.asarray(second_tables()), cross)
    odd = [odd[0]] + [shifted(odd[s], s) for s in range(1, GX)]

    second_table = jnp.asarray(two_parts(basis(NY, YM), 0))
    parts = gram(place, first_table, second_table, odd_weight, even, odd)
    parts = lax.all_to_all(parts, "gy", split_axis=0, concat_axis=0, tiled=True)
    parts = add_parts(parts)
    parts = lax.all_to_all(parts, "gx", split_axis=0, concat_axis=0, tiled=True)
    return analyse(parts, member_order.reshape(M, 1), ensemble)


def solution(mesh):
    placed = (P(None, "gx", "gy"), P(("gx", "gy")), P(("gx", "gy")), P())
    return jax.shard_map(
        on_device, mesh=mesh, in_specs=placed, out_specs=P(None, "gx", "gy"), check_vma=False
    )
```

profile of v0, /device:TPU:0, one launch (start us, length us, event | category | flops | bytes accessed | tf_op | source)
XLA Modules:
  0.0 120.1 jit_solution(7848775746178845738)
XLA Ops:
  0.0 1.2 %copy-done.1 = bf16[8,256,256]{2,1,0:T(8,128)(2,1)S(1)} copy-done((bf16[8,256,256]{2,1,0:T(8,128)(2,1)S(1)}, bf16[8,256,256]{2,1,0:T(8,128)(2,1)}, u32[]{:S(2)}) %copy-start.1) | copy-done | bytes 1048600
  2.6 9.0 %depth_modes.1 = (f32[16,16,16,128]{3,2,1,0:T(8,128)}, f32[8,128]{1,0:T(8,128)}, f32[520,128]{1,0:T(8,128)}, f32[520,128]{1,0:T(8,128)}, f32[520,128]{1,0:T(8,12...) custom-call(s32[1]{0:T(128)} %bitcast.place, ...), custom_call_target="tpu_custom_call" | custom-call | tf_op jit(solution)/shard_map/depth_modes/pallas_call | solution.py:183
  11.6 7.3 %all-to-all-start.1 = ((f32[16,16,16,128]{3,2,1,0:T(8,128)}), f32[16,16,16,128]{3,2,1,0:T(8,128)S(1)}, u32[]{:S(2)}, u32[]{:S(2)}) async-start(f32[16,16,16,128]{3,2,1,0:T(8,128)} %get-tuple-element.32), calls=%async_computation.1 | async-start | bytes 4194304 | tf_op jit(solution)/shard_map/all_to_all | solution.py:501
  18.9 2.0 %collective-permute-start.1 = (f32[520,128]{1,0:T(8,128)}, f32[520,128]{1,0:T(8,128)S(1)}, u32[]{:S(2)}, u32[]{:S(2)}) collective-permute-start(f32[520,128]{1,0:T(8,128)} %get-tuple-element.26), channel_id=1, source_target_pairs={{0,32},{16,48},{32,64},{48,80},{64,96},{80,112},{96,0},{112,16},{1... | collective-permute-start | bytes 798728 | tf_op jit(solution)/shard_map/ppermute | solution.py:486
  20.9 2.9 %collective-permute-start.2 = (f32[520,128]{1,0:T(8,128)}, f32[520,128]{1,0:T(8,128)S(1)}, u32[]{:S(2)}, u32[]{:S(2)}) collective-permute-start(f32[520,128]{1,0:T(8,128)} %get-tuple-element.27), channel_id=1, source_target_pairs={{0,48},{16,64},{32,80},{48,96},{64,112},{80,0},{96,16},{112,32},{1... | collective-permute-start | bytes 798728 | tf_op jit(solution)/shard_map/ppermute | solution.py:486
  23.8 1.2 collective-permute-start.3
  24.9 2.5 %collective-permute-start.4 = (f32[520,128]{1,0:T(8,128)}, f32[520,128]{1,0:T(8,128)S(1)}, u32[]{:S(2)}, u32[]{:S(2)}) collective-permute-start(f32[520,128]{1,0:T(8,128)} %get-tuple-element.29), channel_id=1, source_target_pairs={{0,80},{16,96},{32,112},{48,0},{64,16},{80,32},{96,48},{112,64},{1... | collective-permute-start | bytes 798728 | tf_op jit(solution)/shard_map/ppermute | solution.py:486
  28.0 3.2 %collective-permute-start.5 = (f32[520,128]{1,0:T(8,128)}, f32[520,128]{1,0:T(8,128)S(1)}, u32[]{:S(2)}, u32[]{:S(2)}) collective-permute-start(f32[520,128]{1,0:T(8,128)} %get-tuple-element.30), channel_id=1, source_target_pairs={{0,96},{16,112},{32,0},{48,16},{64,32},{80,48},{96,64},{112,80},{1... | collective-permute-start | bytes 798728 | tf_op jit(solution)/shard_map/ppermute | solution.py:486
  31.2 5.4 %collective-permute-start.6 = (f32[520,128]{1,0:T(8,128)}, f32[520,128]{1,0:T(8,128)S(1)}, u32[]{:S(2)}, u32[]{:S(2)}) collective-permute-start(f32[520,128]{1,0:T(8,128)} %get-tuple-element.31), channel_id=1, source_target_pairs={{0,112},{16,0},{32,16},{48,32},{64,48},{80,64},{96,80},{112,96},{1... | collective-permute-start | bytes 798728 | tf_op jit(solution)/shard_map/ppermute | solution.py:486
  36.6 5.4 %collective-permute-done.2.refs_3_ = f32[520,128]{1,0:T(8,128)S(1)} collective-permute-done((f32[520,128]{1,0:T(8,128)}, f32[520,128]{1,0:T(8,128)S(1)}, u32[]{:S(2)}, u32[]{:S(2)}) %collective-permute-start.2) | collective-permute-done | bytes 266272 | tf_op jit(solution)/shard_map/ppermute | solution.py:486
  42.1 1.2 %collective-permute-done.3.refs_4_ = f32[520,128]{1,0:T(8,128)S(1)} collective-permute-done((f32[520,128]{1,0:T(8,128)}, f32[520,128]{1,0:T(8,128)S(1)}, u32[]{:S(2)}, u32[]{:S(2)}) %collective-permute-start.3) | collective-permute-done | bytes 266272 | tf_op jit(solution)/shard_map/ppermute | solution.py:486
  43.3 1.2 %collective-permute-done.4.refs_5_ = f32[520,128]{1,0:T(8,128)S(1)} collective-permute-done((f32[520,128]{1,0:T(8,128)}, f32[520,128]{1,0:T(8,128)S(1)}, u32[]{:S(2)}, u32[]{:S(2)}) %collective-permute-start.4) | collective-permute-done | bytes 266272 | tf_op jit(solution)/shard_map/ppermute | solution.py:486
  45.2 1.9 %collective-permute-done.6.refs_7_ = f32[520,128]{1,0:T(8,128)S(1)} collective-permute-done((f32[520,128]{1,0:T(8,128)}, f32[520,128]{1,0:T(8,128)S(1)}, u32[]{:S(2)}, u32[]{:S(2)}) %collective-permute-start.6) | collective-permute-done | bytes 266272 | tf_op jit(solution)/shard_map/ppermute | solution.py:486
  47.2 0.9 copy-done.3
  48.1 2.7 %first_modes.1 = f32[16,72,128]{2,1,0:T(8,128)} custom-call(s32[1]{0:T(128)} %bitcast.place, bf16[8,256,128]{2,1,0:T(8,128)(2,1)S(1)} %copy-done, f32[520,128]{1,0:T(8,128)S(1)} %copy-done.3, f32[520,128]{1,0:T(8,128)S(1)} %collective-permute-done.refs_1_, f32[520,128]{1,0:T(8,128)S(1)} %collective-permute-done.1.refs_2_, ...), custom_call_target="tpu_custom_call" | custom-call | tf_op jit(solution)/shard_map/first_modes/pallas_call | solution.py:230
  50.8 7.2 %all-to-all-start = ((f32[16,72,128]{2,1,0:T(8,128)}), f32[16,72,128]{2,1,0:T(8,128)S(1)}, u32[]{:S(2)}, u32[]{:S(2)}) async-start(f32[16,72,128]{2,1,0:T(8,128)} %first_modes.1), calls=%async_computation | async-start | bytes 1179648 | tf_op jit(solution)/shard_map/all_to_all | solution.py:505
  58.0 1.0 copy-done.2
  59.1 1.9 %second_modes.1 = (f32[8,16,128]{2,1,0:T(8,128)}, f32[8,16,128]{2,1,0:T(8,128)}, f32[8,16,128]{2,1,0:T(8,128)}, f32[8,16,128]{2,1,0:T(8,128)}, f32[8,16,128]{2,1...) custom-call(s32[1]{0:T(128)} %bitcast.place, ...), custom_call_target="tpu_custom_call" | custom-call | tf_op jit(solution)/shard_map/second_modes/pallas_call | solution.py:269
  61.0 0.8 collective-permute-start.7
  61.8 1.9 %collective-permute-start.8 = (f32[8,16,128]{2,1,0:T(8,128)}, f32[8,16,128]{2,1,0:T(8,128)S(1)}, u32[]{:S(2)}, u32[]{:S(2)}) collective-permute-start(f32[8,16,128]{2,1,0:T(8,128)} %get-tuple-element.35), channel_id=1, source_target_pairs={{0,32},{16,48},{32,64},{48,80},{64,96},{80,112},{96,0},{112,16},{1... | collective-permute-start | bytes 196616 | tf_op jit(solution)/shard_map/ppermute | solution.py:486
  63.9 2.0 %collective-permute-start.10 = (f32[8,16,128]{2,1,0:T(8,128)}, f32[8,16,128]{2,1,0:T(8,128)S(1)}, u32[]{:S(2)}, u32[]{:S(2)}) collective-permute-start(f32[8,16,128]{2,1,0:T(8,128)} %get-tuple-element.37), channel_id=1, source_target_pairs={{0,64},{16,80},{32,96},{48,112},{64,0},{80,16},{96,32},{112,48},{1... | collective-permute-start | bytes 196616 | tf_op jit(solution)/shard_map/ppermute | solution.py:486
  65.8 2.7 %collective-permute-start.11 = (f32[8,16,128]{2,1,0:T(8,128)}, f32[8,16,128]{2,1,0:T(8,128)S(1)}, u32[]{:S(2)}, u32[]{:S(2)}) collective-permute-start(f32[8,16,128]{2,1,0:T(8,128)} %get-tuple-element.38), channel_id=1, source_target_pairs={{0,80},{16,96},{32,112},{48,0},{64,16},{80,32},{96,48},{112,64},{1... | collective-permute-start | bytes 196616 | tf_op jit(solution)/shard_map/ppermute | solution.py:486
  68.6 1.4 %collective-permute-start.12 = (f32[8,16,128]{2,1,0:T(8,128)}, f32[8,16,128]{2,1,0:T(8,128)S(1)}, u32[]{:S(2)}, u32[]{:S(2)}) collective-permute-start(f32[8,16,128]{2,1,0:T(8,128)} %get-tuple-element.39), channel_id=1, source_target_pairs={{0,96},{16,112},{32,0},{48,16},{64,32},{80,48},{96,64},{112,80},{1... | collective-permute-start | bytes 196616 | tf_op jit(solution)/shard_map/ppermute | solution.py:486
  70.0 1.9 %all-to-all-done.even_ref = f32[16,72,128]{2,1,0:T(8,128)S(1)} async-done(((f32[16,72,128]{2,1,0:T(8,128)}), f32[16,72,128]{2,1,0:T(8,128)S(1)}, u32[]{:S(2)}, u32[]{:S(2)}) %all-to-all-start) | async-done | bytes 589856 | tf_op jit(solution)/shard_map/all_to_all | solution.py:505
  71.8 1.2 %collective-permute-done.12.refs_6_ = f32[8,16,128]{2,1,0:T(8,128)S(1)} collective-permute-done((f32[8,16,128]{2,1,0:T(8,128)}, f32[8,16,128]{2,1,0:T(8,128)S(1)}, u32[]{:S(2)}, u32[]{:S(2)}) %collective-permute-start.12) | collective-permute-done | bytes 65568 | tf_op jit(solution)/shard_map/ppermute | solution.py:486
  73.1 0.8 copy-done.5
  73.9 1.8 %gram.1 = f32[16,32,128]{2,1,0:T(8,128)} custom-call(s32[1]{0:T(128)} %bitcast.place, bf16[8,256,128]{2,1,0:T(8,128)(2,1)S(1)} %copy-done, bf16[128,256]{1,0:T(8,128)(2,1)S(1)} %copy-done.4, f32[8,128]{1,0:T(8,128)S(1)} %copy-done.6, f32[16,72,128]{2,1,0:T(8,128)S(1)} %all-to-all-done.even_ref, f32[8,16,128]{2,1,0:T(8,128)S(1)} %copy-done.5, ...), custom_call_target="tpu_custom_call" | custom-call | tf_op jit(solution)/shard_map/gram/pallas_call | solution.py:348
  75.7 16.4 %all_to_all.20.parts = f32[16,32,128]{2,1,0:T(8,128)} all-to-all(f32[16,32,128]{2,1,0:T(8,128)} %gram.1), channel_id=1, replica_groups=mesh['gx'=8,'gy'=16] {'gy'}, dimensions={0} | all-to-all | bytes 524288 | tf_op jit(solution)/shard_map/all_to_all | solution.py:511
  92.1 1.6 %add_parts.1 = f32[8,32,128]{2,1,0:T(8,128)} custom-call(f32[16,32,128]{2,1,0:T(8,128)} %all_to_all.20.parts), custom_call_target="tpu_custom_call" | custom-call | tf_op jit(solution)/shard_map/add_parts/pallas_call | solution.py:364
  93.7 4.0 %all-to-all-start.3 = ((f32[8,32,128]{2,1,0:T(8,128)}), f32[8,32,128]{2,1,0:T(8,128)S(1)}, u32[]{:S(2)}, u32[]{:S(2)}) async-start(f32[8,32,128]{2,1,0:T(8,128)} %add_parts.1), calls=%async_computation.3 | async-start | bytes 262144 | tf_op jit(solution)/shard_map/all_to_all | solution.py:513
  97.8 6.0 %all-to-all-done.3.parts = f32[8,32,128]{2,1,0:T(8,128)S(1)} async-done(((f32[8,32,128]{2,1,0:T(8,128)}), f32[8,32,128]{2,1,0:T(8,128)S(1)}, u32[]{:S(2)}, u32[]{:S(2)}) %all-to-all-start.3) | async-done | bytes 131104 | tf_op jit(solution)/shard_map/all_to_all | solution.py:513
  103.9 16.2 %analysis.1 = f32[64,32,1024]{2,1,0:T(8,128)} custom-call(f32[8,32,128]{2,1,0:T(8,128)S(1)} %all-to-all-done.3.parts, s32[64,1]{1,0:T(8,128)S(1)} %copy.9.order, f32[64,32,1024]{2,1,0:T(8,128)} %ens_hbm.1), custom_call_target="tpu_custom_call" | custom-call | tf_op jit(solution)/shard_map/analysis/pallas_call | solution.py:464
  (30 shorter events, 3.0 us)
Async XLA Ops:
  0.0 1.2 %copy-start.1 = (bf16[8,256,256]{2,1,0:T(8,128)(2,1)S(1)}, bf16[8,256,256]{2,1,0:T(8,128)(2,1)}, u32[]{:S(2)}) copy-start(bf16[8,256,256]{2,1,0:T(8,128)(2,1)} %constant.15.clone.refs_8_) | copy-start | bytes 3145732
  1.2 0.7 copy-start.7
  1.9 0.7 copy-start.8
  2.6 44.6 %copy-start = (bf16[8,256,128]{2,1,0:T(8,128)(2,1)S(1)}, bf16[8,256,128]{2,1,0:T(8,128)(2,1)}, u32[]{:S(2)}) copy-start(bf16[8,256,128]{2,1,0:T(8,128)(2,1)} %constant.14.clone.table_ref.first_table) | copy-start | bytes 1572868
  11.6 61.5 %copy-start.4 = (bf16[128,256]{1,0:T(8,128)(2,1)S(1)}, bf16[128,256]{1,0:T(8,128)(2,1)}, u32[]{:S(2)}) copy-start(bf16[128,256]{1,0:T(8,128)(2,1)} %constant.17.clone.second_table) | copy-start | bytes 196612
  11.6 61.5 %copy-start.6 = (f32[8,128]{1,0:T(8,128)S(1)}, f32[8,128]{1,0:T(8,128)}, u32[]{:S(2)}) copy-start(f32[8,128]{1,0:T(8,128)} %get-tuple-element.23.odd_weight) | copy-start | bytes 12292
  11.6 86.1 %copy-start.9 = (s32[64]{0:T(128)S(1)}, s32[64]{0:T(128)}, u32[]{:S(2)}) copy-start(s32[64]{0:T(128)} %param.11) | copy-start | bytes 772
  11.6 39.2 %all-to-all-start.1 = ((f32[16,16,16,128]{3,2,1,0:T(8,128)}), f32[16,16,16,128]{3,2,1,0:T(8,128)S(1)}, u32[]{:S(2)}, u32[]{:S(2)}) async-start(f32[16,16,16,128]{3,2,1,0:T(8,128)} %get-tuple-element.32), calls=%async_computation.1 | async-start | bytes 4194304 | tf_op jit(solution)/shard_map/all_to_all | solution.py:501
  18.9 9.1 %collective-permute-start = (f32[520,128]{1,0:T(8,128)}, f32[520,128]{1,0:T(8,128)S(1)}, u32[]{:S(2)}, u32[]{:S(2)}) collective-permute-start(f32[520,128]{1,0:T(8,128)} %get-tuple-element.25), channel_id=1, source_target_pairs={{0,16},{16,32},{32,48},{48,64},{64,80},{80,96},{96,112},{112,0},{1... | collective-permute-start | bytes 798728 | tf_op jit(solution)/shard_map/ppermute | solution.py:486
  18.9 12.3 %collective-permute-start.1 = (f32[520,128]{1,0:T(8,128)}, f32[520,128]{1,0:T(8,128)S(1)}, u32[]{:S(2)}, u32[]{:S(2)}) collective-permute-start(f32[520,128]{1,0:T(8,128)} %get-tuple-element.26), channel_id=1, source_target_pairs={{0,32},{16,48},{32,64},{48,80},{64,96},{80,112},{96,0},{112,16},{1... | collective-permute-start | bytes 798728 | tf_op jit(solution)/shard_map/ppermute | solution.py:486
  20.9 21.2 %collective-permute-start.2 = (f32[520,128]{1,0:T(8,128)}, f32[520,128]{1,0:T(8,128)S(1)}, u32[]{:S(2)}, u32[]{:S(2)}) collective-permute-start(f32[520,128]{1,0:T(8,128)} %get-tuple-element.27), channel_id=1, source_target_pairs={{0,48},{16,64},{32,80},{48,96},{64,112},{80,0},{96,16},{112,32},{1... | collective-permute-start | bytes 798728 | tf_op jit(solution)/shard_map/ppermute | solution.py:486
  23.8 19.5 %collective-permute-start.3 = (f32[520,128]{1,0:T(8,128)}, f32[520,128]{1,0:T(8,128)S(1)}, u32[]{:S(2)}, u32[]{:S(2)}) collective-permute-start(f32[520,128]{1,0:T(8,128)} %get-tuple-element.28), channel_id=1, source_target_pairs={{0,64},{16,80},{32,96},{48,112},{64,0},{80,16},{96,32},{112,48},{1... | collective-permute-start | bytes 798728 | tf_op jit(solution)/shard_map/ppermute | solution.py:486
  24.9 19.5 %collective-permute-start.4 = (f32[520,128]{1,0:T(8,128)}, f32[520,128]{1,0:T(8,128)S(1)}, u32[]{:S(2)}, u32[]{:S(2)}) collective-permute-start(f32[520,128]{1,0:T(8,128)} %get-tuple-element.29), channel_id=1, source_target_pairs={{0,80},{16,96},{32,112},{48,0},{64,16},{80,32},{96,48},{112,64},{1... | collective-permute-start | bytes 798728 | tf_op jit(solution)/shard_map/ppermute | solution.py:486
  28.0 17.2 %collective-permute-start.5 = (f32[520,128]{1,0:T(8,128)}, f32[520,128]{1,0:T(8,128)S(1)}, u32[]{:S(2)}, u32[]{:S(2)}) collective-permute-start(f32[520,128]{1,0:T(8,128)} %get-tuple-element.30), channel_id=1, source_target_pairs={{0,96},{16,112},{32,0},{48,16},{64,32},{80,48},{96,64},{112,80},{1... | collective-permute-start | bytes 798728 | tf_op jit(solution)/shard_map/ppermute | solution.py:486
  31.2 15.9 %collective-permute-start.6 = (f32[520,128]{1,0:T(8,128)}, f32[520,128]{1,0:T(8,128)S(1)}, u32[]{:S(2)}, u32[]{:S(2)}) collective-permute-start(f32[520,128]{1,0:T(8,128)} %get-tuple-element.31), channel_id=1, source_target_pairs={{0,112},{16,0},{32,16},{48,32},{64,48},{80,64},{96,80},{112,96},{1... | collective-permute-start | bytes 798728 | tf_op jit(solution)/shard_map/ppermute | solution.py:486
  47.2 1.0 copy-start.3
  50.8 21.0 %all-to-all-start = ((f32[16,72,128]{2,1,0:T(8,128)}), f32[16,72,128]{2,1,0:T(8,128)S(1)}, u32[]{:S(2)}, u32[]{:S(2)}) async-start(f32[16,72,128]{2,1,0:T(8,128)} %first_modes.1), calls=%async_computation | async-start | bytes 1179648 | tf_op jit(solution)/shard_map/all_to_all | solution.py:505
  58.0 1.0 copy-start.2
  61.0 7.6 %collective-permute-start.7 = (f32[8,16,128]{2,1,0:T(8,128)}, f32[8,16,128]{2,1,0:T(8,128)S(1)}, u32[]{:S(2)}, u32[]{:S(2)}) collective-permute-start(f32[8,16,128]{2,1,0:T(8,128)} %get-tuple-element.34), channel_id=1, source_target_pairs={{0,16},{16,32},{32,48},{48,64},{64,80},{80,96},{96,112},{112,0},{1... | collective-permute-start | bytes 196616 | tf_op jit(solution)/shard_map/ppermute | solution.py:486
  61.8 8.2 %collective-permute-start.8 = (f32[8,16,128]{2,1,0:T(8,128)}, f32[8,16,128]{2,1,0:T(8,128)S(1)}, u32[]{:S(2)}, u32[]{:S(2)}) collective-permute-start(f32[8,16,128]{2,1,0:T(8,128)} %get-tuple-element.35), channel_id=1, source_target_pairs={{0,32},{16,48},{32,64},{48,80},{64,96},{80,112},{96,0},{112,16},{1... | collective-permute-start | bytes 196616 | tf_op jit(solution)/shard_map/ppermute | solution.py:486
  63.7 8.1 %collective-permute-start.9 = (f32[8,16,128]{2,1,0:T(8,128)}, f32[8,16,128]{2,1,0:T(8,128)S(1)}, u32[]{:S(2)}, u32[]{:S(2)}) collective-permute-start(f32[8,16,128]{2,1,0:T(8,128)} %get-tuple-element.36), channel_id=1, source_target_pairs={{0,48},{16,64},{32,80},{48,96},{64,112},{80,0},{96,16},{112,32},{1... | collective-permute-start | bytes 196616 | tf_op jit(solution)/shard_map/ppermute | solution.py:486
  63.9 8.0 %collective-permute-start.10 = (f32[8,16,128]{2,1,0:T(8,128)}, f32[8,16,128]{2,1,0:T(8,128)S(1)}, u32[]{:S(2)}, u32[]{:S(2)}) collective-permute-start(f32[8,16,128]{2,1,0:T(8,128)} %get-tuple-element.37), channel_id=1, source_target_pairs={{0,64},{16,80},{32,96},{48,112},{64,0},{80,16},{96,32},{112,48},{1... | collective-permute-start | bytes 196616 | tf_op jit(solution)/shard_map/ppermute | solution.py:486
  65.8 6.0 %collective-permute-start.11 = (f32[8,16,128]{2,1,0:T(8,128)}, f32[8,16,128]{2,1,0:T(8,128)S(1)}, u32[]{:S(2)}, u32[]{:S(2)}) collective-permute-start(f32[8,16,128]{2,1,0:T(8,128)} %get-tuple-element.38), channel_id=1, source_target_pairs={{0,80},{16,96},{32,112},{48,0},{64,16},{80,32},{96,48},{112,64},{1... | collective-permute-start | bytes 196616 | tf_op jit(solution)/shard_map/ppermute | solution.py:486
  68.6 4.5 %collective-permute-start.12 = (f32[8,16,128]{2,1,0:T(8,128)}, f32[8,16,128]{2,1,0:T(8,128)S(1)}, u32[]{:S(2)}, u32[]{:S(2)}) collective-permute-start(f32[8,16,128]{2,1,0:T(8,128)} %get-tuple-element.39), channel_id=1, source_target_pairs={{0,96},{16,112},{32,0},{48,16},{64,32},{80,48},{96,64},{112,80},{1... | collective-permute-start | bytes 196616 | tf_op jit(solution)/shard_map/ppermute | solution.py:486
  70.0 3.1 %collective-permute-start.13 = (f32[8,16,128]{2,1,0:T(8,128)}, f32[8,16,128]{2,1,0:T(8,128)S(1)}, u32[]{:S(2)}, u32[]{:S(2)}) collective-permute-start(f32[8,16,128]{2,1,0:T(8,128)} %get-tuple-element.40), channel_id=1, source_target_pairs={{0,112},{16,0},{32,16},{48,32},{64,48},{80,64},{96,80},{112,96},{1... | collective-permute-start | bytes 196616 | tf_op jit(solution)/shard_map/ppermute | solution.py:486
  73.1 0.8 copy-start.5
  93.7 10.1 %all-to-all-start.3 = ((f32[8,32,128]{2,1,0:T(8,128)}), f32[8,32,128]{2,1,0:T(8,128)S(1)}, u32[]{:S(2)}, u32[]{:S(2)}) async-start(f32[8,32,128]{2,1,0:T(8,128)} %add_parts.1), calls=%async_computation.3 | async-start | bytes 262144 | tf_op jit(solution)/shard_map/all_to_all | solution.py:513
where the time goes:
time: 121 us; the launch traced here: 120 us
  starting transfers between devices  44.6 us (37%)
  Pallas kernels  33.3 us (28%)
  waiting for transfers between devices  20.2 us (17%)
  blocking collectives  16.4 us (14%)
  local copies, waits for them, and re-layouts  5.53 us (5%)
    ppermute x14, starting transfers between devices, shifted(): return lax.ppermute(block, 'gx', [(i, (i + shift) % GX) for i in range(GX)])  26.2 us
    all_to_all x1, blocking collectives, on_device(): parts = lax.all_to_all(parts, 'gy', split_axis=0, concat_axis=0, tiled=True)  16.4 us
    pallas_call x1, Pallas kernels, analyse(): pl.pallas_call(analysis_kernel, in_specs=[pl.BlockSpec(memory_space=pltpu...  16.2 us
    ppermute x14, waiting for transfers between devices, shifted(): return lax.ppermute(block, 'gx', [(i, (i + shift) % GX) for i in range(GX)])  12.3 us
    pallas_call x1, Pallas kernels, depth_modes(): pl.pallas_call(depth_kernel, grid_spec=grid_spec, out_shape=[pltpu.HBM((G...  8.97 us
    all_to_all x1, starting transfers between devices, on_device(): cross = lax.all_to_all(cross, 'gy', split_axis=0, concat_axis=0, tiled=True)  7.27 us
    all_to_all x1, starting transfers between devices, on_device(): even = lax.all_to_all(even, 'gy', split_axis=0, concat_axis=0, tiled=True)  7.2 us
    all_to_all x1, waiting for transfers between devices, on_device(): parts = lax.all_to_all(parts, 'gx', split_axis=0, concat_axis=0, tiled=True)  6.03 us
  transfers between devices with their start and end apart: 17, of which 9 were waited for; matrix products, arithmetic and copies ran while one was open for 0% of the time, Pallas kernels for 4%

commit v1 on v0

v1 whole, which is shorter than its diff:
```python
import math

import jax
import jax.numpy as jnp
import numpy as np
from jax import lax
from jax.experimental import pallas as pl
from jax.experimental.pallas import tpu as pltpu
from jax.sharding import PartitionSpec as P

M = 64
NX = 256
NY = 256
NZ = 64
XM = 64
YM = 64
ZM = 32
NS_ITERS = 18
OBS_DEV = 512
GX = 8
GY = 16
LX = NX // GX
LY = NY // GY

exact_mode = lax.Precision.HIGHEST
f32 = jnp.float32
bf16 = jnp.bfloat16


def basis(length, count):
    q = np.arange(length)
    r = np.arange(count)
    half = count // 2
    freq = np.where(r < half, r, r - half + 1)
    phase = (freq[:, None] * q[None, :] % length) * (2.0 * math.pi / length)
    scale = np.where(r == 0, math.sqrt(1.0 / length), math.sqrt(2.0 / length))
    return scale[:, None] * np.where((r < half)[:, None], np.cos(phase), np.sin(phase))


def two_parts(table, axis):
    high = table.astype(np.float32).astype(jnp.bfloat16)
    low = (table - high.astype(np.float64)).astype(np.float32).astype(jnp.bfloat16)
    return np.concatenate([high, low], axis=axis)


def depth_tables():
    bz = basis(NZ, ZM)
    out = np.zeros((GX, 128, 256))
    for g in range(GX):
        for y4 in range(4):
            cols = slice(64 * y4, 64 * y4 + 64)
            for h in range(GY):
                out[g, 16 * y4 + h, cols] = bz[2 * h + 1]
            for s in range(GX):
                for c2 in range(2):
                    out[g, 64 + 8 * s + 2 * y4 + c2, cols] = bz[4 * ((g + s) % GX) + 2 * c2]
    return two_parts(out.transpose(0, 2, 1), 2)


def first_tables():
    bx = basis(NX, XM)
    out = np.zeros((GX, XM, 2, GX, LX // 2))
    for g in range(GX):
        for s in range(GX):
            start = LX * ((g - s) % GX)
            block = bx[:, start : start + LX]
            out[g, :, 0, s, :] = block[:, 0::2]
            out[g, :, 1, s, :] = block[:, 1::2]
    return two_parts(out.reshape(GX, XM, NX), 1)


def second_table():
    high, low = np.split(two_parts(basis(NY, YM), 0), 2)
    return np.stack([np.concatenate([part, part]) for part in (high, low)]).astype(np.float32)


def from_row(table, start):
    return jnp.concatenate([table[part, pl.ds(start, YM), :] for part in range(2)]).astype(bf16)


def split(value):
    high = value.astype(bf16)
    return high, (value - high.astype(f32)).astype(bf16)


def three_parts(value):
    high = value.astype(bf16)
    rest = value - high.astype(f32)
    middle = rest.astype(bf16)
    return high, middle, (rest - middle.astype(f32)).astype(bf16)


def contract(table, value):
    rows = table.shape[0] // 2
    high, low = split(value)
    first = jnp.dot(table, high, preferred_element_type=f32)
    second = jnp.dot(table[:rows], low, preferred_element_type=f32)
    return first[:rows] + first[rows:] + second


NT = ((1,), (1,))


SCALAR = pl.BlockSpec(memory_space=pltpu.SMEM)
WHOLE = pl.BlockSpec(memory_space=pltpu.VMEM)


def half_lanes(shape):
    return lax.broadcasted_iota(jnp.int32, shape, 1) < 64


def unpair(one, two):
    left = half_lanes(one.shape)
    return jnp.concatenate(
        [
            jnp.where(left, one, pltpu.roll(two, 64, 1)),
            jnp.where(left, pltpu.roll(one, 64, 1), two),
        ]
    )


def mode_weights(index, scale):
    square = scale * (1.0 / math.sqrt(M - 1))
    square = square * square
    high = lax.broadcasted_iota(jnp.int32, (16, OBS_DEV), 0) == (index >> 6)
    low = lax.broadcasted_iota(jnp.int32, (XM, OBS_DEV), 0) == (index & 63)
    parts = jnp.concatenate(
        [jnp.where(high, part.astype(f32), 0.0) for part in three_parts(square)]
    ).astype(bf16)
    sums = lax.dot_general(
        parts, low.astype(f32).astype(bf16), (NT, ((), ())), preferred_element_type=f32
    )
    return sums[:16] + sums[16:32] + sums[32:]


def one_row(ref):
    return jnp.concatenate([ref[i : i + 1, :] for i in range(OBS_DEV // 128)], axis=1)


def depth_kernel(place, ens, table_ref, index, scale, cross_ref, odd_weight, *refs):
    del place
    row_refs, held = refs[:GX], refs[GX]
    step = pl.program_id(0)

    @pl.when(step == 0)
    def _():
        weight = mode_weights(one_row(index), one_row(scale))
        weight = jnp.concatenate([weight, jnp.zeros((16, 64), f32)], axis=1)
        odd_weight[...] = weight[8:]
        for ref in row_refs:
            ref[512:520, :] = weight[:8]

    cross = cross_ref.reshape(GY * 4 * LY, 128)
    table = table_ref[0]
    for quad in range(4):
        lanes = slice(256 * quad, 256 * quad + 256)
        block = ens[:, :, lanes]
        block = (block - jnp.sum(block, axis=0, keepdims=True) * (1.0 / M)).reshape(M * 8, 256)
        high, low = split(block)
        first = jnp.dot(high, table, preferred_element_type=f32)
        second = jnp.dot(low, table[:, :128], preferred_element_type=f32)
        held[quad] = first[:, :128] + first[:, 128:] + second
        for p in range(4):
            modes = jnp.concatenate(
                [held[quad, pl.ds(2 * p + parity, M, stride=8), :] for parity in range(2)]
            ).T
            for y4 in range(4):
                cross[pl.ds(LY * p + 4 * quad + y4, GY, stride=4 * LY), :] = modes[
                    16 * y4 : 16 * y4 + 16
                ]
            for shift in range(GX):
                start = pl.multiple_of(128 * step + 32 * p + 8 * quad, 8)
                row_refs[shift][pl.ds(start, 8), :] = modes[64 + 8 * shift : 72 + 8 * shift]


def depth_modes(place, ensemble, tables, index, scale):
    grid_spec = pltpu.PrefetchScalarGridSpec(
        num_scalar_prefetch=1,
        grid=(LX // 8,),
        in_specs=[pl.BlockSpec((M, 8, LY * NZ), lambda i, place: (0, i, 0))]
        + [pl.BlockSpec((1, 256, 256), lambda i, place: (place[0], 0, 0))]
        + [pl.BlockSpec((OBS_DEV // 128, 128), lambda i, place: (0, 0))] * 2,
        out_specs=[
            pl.BlockSpec((GY, 4, LY, 128), lambda i, place: (0, i, 0, 0)),
            pl.BlockSpec((8, 128), lambda i, place: (0, 0)),
        ]
        + [pl.BlockSpec((520, 128), lambda i, place: (0, 0))] * GX,
        scratch_shapes=[pltpu.VMEM((4, M * 8, 128), f32)],
    )
    return pl.pallas_call(
        depth_kernel,
        grid_spec=grid_spec,
        out_shape=[pltpu.HBM((GY, LX // 2, LY, 128), f32)]
        + [jax.ShapeDtypeStruct(shape, f32) for shape in ((8, 128), (520, 128))]
        + [pltpu.HBM((520, 128), f32)] * (GX - 1),
        compiler_params=pltpu.CompilerParams(vmem_limit_bytes=48 << 20),
        name="depth_modes",
    )(place, ensemble, tables, index, scale)


def first_kernel(place, table_ref, *refs):
    blocks, out_ref, held = refs[:GX], refs[GX], refs[GX + 1]
    out = out_ref.reshape(XM * 18, 128)
    held[64:, :] = jnp.zeros((64, 128), f32)
    for shift in range(GX):
        start = pl.multiple_of(8 * ((place[0] + GX - shift) % GX), 8)
        held[pl.ds(start, 8), :] = blocks[shift][512:520, :]
    out[pl.ds(16, XM, stride=18), :] = held[...].T[:64]
    out[pl.ds(17, XM, stride=18), :] = jnp.zeros((XM, 128), f32)
    table = table_ref[place[0]]
    for y in range(0, LY, 2):
        value = [
            unpair(
                *[
                    jnp.concatenate([b[pl.ds(2 * k + c2, 16, stride=32), :] for b in blocks])
                    for c2 in range(2)
                ]
            )
            for k in (y, y + 1)
        ]
        modes = contract(table, jnp.concatenate(value, axis=1))
        for k in range(2):
            out[pl.ds(y + k, XM, stride=18), :] = modes[:, 128 * k : 128 * k + 128]


def first_modes(place, tables, blocks):
    return pl.pallas_call(
        first_kernel,
        in_specs=[SCALAR] + [WHOLE] * (GX + 1),
        out_specs=WHOLE,
        out_shape=pltpu.HBM((GY, 72, 128), f32),
        scratch_shapes=[pltpu.VMEM((128, 128), f32)],
        compiler_params=pltpu.CompilerParams(vmem_limit_bytes=16 << 20),
        name="first_modes",
    )(place, tables, *blocks)


def second_kernel(place, table_ref, cross, *outs):
    table = from_row(table_ref, pl.multiple_of(8 * place[0], 8))
    for group in range(LX // 4):
        value = jnp.concatenate(
            [
                jnp.concatenate([cross[h, 2 * group + pair] for h in range(GY)])
                for pair in range(2)
            ],
            axis=1,
        )
        modes = contract(table, value)
        for pair in range(2):
            for shift in range(GX):
                outs[shift].reshape(128, 128)[
                    pl.ds(2 * group + pair, 8, stride=16), :
                ] = modes[8 * shift : 8 * shift + 8, 128 * pair : 128 * pair + 128]


def second_modes(place, tables, cross):
    return pl.pallas_call(
        second_kernel,
        in_specs=[SCALAR, WHOLE, WHOLE],
        out_specs=[WHOLE] * GX,
        out_shape=[jax.ShapeDtypeStruct((8, 16, 128), f32)]
        + [pltpu.HBM((8, 16, 128), f32)] * (GX - 1),
        compiler_params=pltpu.CompilerParams(vmem_limit_bytes=16 << 20),
        name="second_modes",
    )(place, tables, cross)


def gram_kernel(place, first_table, table_ref, odd_weight, even_ref, *refs):
    odd_refs, out = refs[:GX], refs[GX]
    total = jnp.zeros((128, 128), f32)

    def add(rows, one, two):
        top = lax.broadcasted_iota(jnp.int32, (128, 256), 0) < 64
        weight = jnp.where(top, jnp.concatenate(one, axis=1), jnp.concatenate(two, axis=1))
        return jnp.dot(
            rows.T * weight, rows, precision=exact_mode, preferred_element_type=f32
        )

    table = from_row(table_ref, 0)
    rows = []
    for pair in range(2):
        value = jnp.concatenate(
            [
                jnp.concatenate([even_ref[h, 18 * a : 18 * a + 16] for h in range(GY)])
                for a in (2 * pair, 2 * pair + 1)
            ],
            axis=1,
        )
        modes = contract(table, value)
        rows += [modes[:, :128], modes[:, 128:]]
    weights = [
        [even_ref[2 * place[0] + c2, 18 * a + 16 : 18 * a + 17, :64] for a in range(4)]
        for c2 in range(2)
    ]
    total += add(jnp.concatenate(rows), *weights)
    table = first_table[place[0]]
    rows = []
    for b in range(0, 8, 4):
        value = [
            unpair(*[jnp.concatenate([ref[k + b2] for ref in odd_refs]) for b2 in range(2)])
            for k in (b, b + 2)
        ]
        modes = contract(table, jnp.concatenate(value, axis=1))
        rows += [modes[:, :128], modes[:, 128:]]
    weights = [[odd_weight[b : b + 1, :64] for b in range(b2, 8, 2)] for b2 in range(2)]
    total += add(jnp.concatenate(rows), *weights)
    gram = total[:64] + pltpu.roll(total[64:], 64, 1)
    packed = jnp.where(half_lanes((32, 128)), gram[:32], pltpu.roll(gram[32:], 64, 1))
    for i in range(GX):
        out[i] = packed


def gram(place, first_table, second_table, odd_weight, even, odd):
    return pl.pallas_call(
        gram_kernel,
        in_specs=[SCALAR] + [WHOLE] * (GX + 4),
        out_specs=WHOLE,
        out_shape=jax.ShapeDtypeStruct((GX, 32, 128), f32),
        compiler_params=pltpu.CompilerParams(vmem_limit_bytes=16 << 20),
        name="gram",
    )(place, first_table, second_table, odd_weight, even, *odd)


def exact_dot(one, two):
    a, b, c = three_parts(one)
    d, e, f = three_parts(two)
    first = jnp.dot(jnp.concatenate([a, b, c]), d, preferred_element_type=f32)
    second = jnp.dot(jnp.concatenate([a, b]), e, preferred_element_type=f32)
    third = jnp.dot(a, f, preferred_element_type=f32)
    return first[:M] + (second[:M] + first[M : 2 * M]) + (first[2 * M :] + second[M:] + third)


def combine_table(parts, order, beside):
    packed = jnp.sum(parts, axis=0)
    row = lax.broadcasted_iota(jnp.int32, (M, M), 0)
    column = lax.broadcasted_iota(jnp.int32, (M, M), 1)
    identity = (row == column).astype(f32)
    matrix = identity + jnp.concatenate([packed[:, :64], packed[:, 64:]])
    squares = jnp.sum(jnp.sum(matrix * matrix, axis=1, keepdims=True), axis=0, keepdims=True)
    frobenius = jnp.sqrt(squares)

    def sweep(turn, carry):
        root, inverse = carry
        change = 1.5 * identity - 0.5 * exact_dot(inverse, root)
        return exact_dot(root, change), exact_dot(change, inverse)

    def sweep_beside(turn, carry):
        beside(turn)
        return sweep(turn, carry)

    carry = lax.fori_loop(0, 16, sweep_beside, (matrix / frobenius, identity))
    _, inverse = lax.fori_loop(16, NS_ITERS, sweep, carry)
    transform = inverse / jnp.sqrt(frobenius)
    chosen = (order == row).astype(f32).T
    weight = lax.dot_general(
        chosen, transform, (NT, ((), ())), precision=exact_mode, preferred_element_type=f32
    )
    high, low = split(weight)
    high, low = high.astype(f32), low.astype(f32)
    none = jnp.zeros((M, M), f32)
    return jnp.concatenate(
        [
            jnp.concatenate([high, high, none, none], axis=1),
            jnp.concatenate([low, none, none, none], axis=1),
            jnp.concatenate([none, none, high, high], axis=1),
            jnp.concatenate([none, none, low, none], axis=1),
        ]
    ).astype(bf16)


def analysis_kernel(parts, order, ens_hbm, out_hbm, ens, ready, out, weights, fetched, stored):
    def fetch(n):
        i, t = n // 8, n % 8
        place = (slice(None), pl.ds(8 * i, 8), pl.ds(128 * t, 128))
        return pltpu.make_async_copy(ens_hbm.at[place], ens.at[n], fetched.at[n])

    def store(n):
        i, t = n // 8, n % 8
        place = (slice(None), pl.ds(8 * i, 8), pl.ds(128 * t, 128))
        return pltpu.make_async_copy(out.at[n], out_hbm.at[place], stored.at[n])

    count = LX * LY * NZ // 1024
    for n in range(count):
        fetch(n).start()

    def prepare(pair):
        tiles = (2 * pair, 2 * pair + 1)
        for n in tiles:
            fetch(n).wait()
        means = [jnp.sum(ens[n], axis=0) * (1.0 / M) for n in tiles]
        flats = [ens.at[n].reshape(M * 8, 128) for n in tiles]
        for x in range(8):
            high, low = split(
                jnp.concatenate(
                    [flats[k][pl.ds(x, M, stride=8), :] - means[k][x : x + 1] for k in range(2)],
                    axis=1,
                )
            )
            ready[4 * pair + x // 2, 128 * (x % 2) : 128 * (x % 2) + 64] = high
            ready[4 * pair + x // 2, 128 * (x % 2) + 64 : 128 * (x % 2) + 128] = low

    weights[...] = combine_table(parts[...], order[...], prepare)

    @pl.loop(0, LX // 8)
    def _(group):
        table = weights[...]
        for pair in range(4):
            tiles = (8 * group + 2 * pair, 8 * group + 2 * pair + 1)
            outs = [out.at[n].reshape(M * 8, 128) for n in tiles]
            for x in range(0, 8, 2):
                result = jnp.dot(
                    table, ready[16 * group + 4 * pair + x // 2], preferred_element_type=f32
                )
                for i in range(2):
                    sums = result[128 * i : 128 * i + 64] + result[128 * i + 64 : 128 * i + 128]
                    for k in range(2):
                        outs[k][pl.ds(x + i, M, stride=8), :] = sums[:, 128 * k : 128 * k + 128]
            for n in tiles:
                store(n).start()

    for n in range(count):
        store(n).wait()


def analyse(parts, order, ensemble):
    count = LX * LY * NZ // 1024
    return pl.pallas_call(
        analysis_kernel,
        in_specs=[
            pl.BlockSpec(memory_space=pltpu.VMEM),
            pl.BlockSpec(memory_space=pltpu.VMEM),
            pl.BlockSpec(memory_space=pl.ANY),
        ],
        out_specs=pl.BlockSpec(memory_space=pl.ANY),
        out_shape=jax.ShapeDtypeStruct((M, LX, LY * NZ), f32),
        scratch_shapes=[
            pltpu.VMEM((count, M, 8, 128), f32),
            pltpu.VMEM((2 * count, 256, 256), bf16),
            pltpu.VMEM((count, M, 8, 128), f32),
            pltpu.VMEM((256, 256), bf16),
            pltpu.SemaphoreType.DMA((count,)),
            pltpu.SemaphoreType.DMA((count,)),
        ],
        compiler_params=pltpu.CompilerParams(vmem_limit_bytes=40 << 20),
        name="analysis",
    )(parts, order, ensemble)


def shifted(block, shift):
    return lax.ppermute(block, "gx", [(i, (i + shift) % GX) for i in range(GX)])


def on_device(ensemble, obs_index, obs_scale, member_order):
    gx = lax.axis_index("gx")
    place = gx.astype(jnp.int32).reshape(1)
    ensemble = pltpu.with_memory_space_constraint(ensemble, pltpu.HBM)
    in_hbm = lambda table: pltpu.with_memory_space_constraint(jnp.asarray(table), pltpu.HBM)
    first_table = jnp.asarray(first_tables())
    y_table = jnp.asarray(second_table())
    cross, odd_weight, *rows = depth_modes(
        place,
        ensemble,
        in_hbm(depth_tables()),
        in_hbm(obs_index.reshape(OBS_DEV // 128, 128)),
        in_hbm(obs_scale.reshape(OBS_DEV // 128, 128)),
    )
    cross = lax.all_to_all(cross, "gy", split_axis=0, concat_axis=0, tiled=True)
    rows = [rows[0]] + [shifted(rows[s], s) for s in range(1, GX)]
    even = first_modes(place, first_table, rows)
    odd = second_modes(place, y_table, cross)
    even = lax.all_to_all(even, "gy", split_axis=0, concat_axis=0, tiled=True)
    odd = [odd[0]] + [shifted(odd[s], s) for s in range(1, GX)]
    parts = gram(place, first_table, y_table, odd_weight, even, odd)
    parts = lax.all_to_all(parts, "gx", split_axis=0, concat_axis=0, tiled=True)
    parts = jnp.broadcast_to(jnp.sum(parts, axis=0), (GY, 32, 128))
    parts = lax.all_to_all(parts, "gy", split_axis=0, concat_axis=0, tiled=True)
    return analyse(parts, member_order.reshape(1, M), ensemble)


def solution(mesh):
    placed = (P(None, "gx", "gy"), P(("gx", "gy")), P(("gx", "gy")), P())
    return jax.shard_map(
        on_device, mesh=mesh, in_specs=placed, out_specs=P(None, "gx", "gy"), check_vma=False
    )
```

time: 121 us -> 107 us (0.88)
  blocking collectives: 16.4 us -> 25 us
  Pallas kernels: 33.3 us -> 26.1 us
  local copies, waits for them, and re-layouts: 5.53 us -> 0.03 us
  waiting for transfers between devices: 20.2 us -> 15.3 us
  starting transfers between devices: 44.6 us -> 39.8 us
    all_to_all x0 -> x1, blocking collectives: none -> 9.46 us  [on_device(): parts = lax.all_to_all(parts, 'gx', split_axis=0, concat_axis=0, tiled=True)]
    all_to_all x1 -> x0, waiting for transfers between devices: 6.03 us -> none  [on_device(): parts = lax.all_to_all(parts, 'gx', split_axis=0, concat_axis=0, tiled=True)]
    unnamed x20 -> x6, local copies, waits for them, and re-layouts: 5.43 us -> 0.01 us
    all_to_all x1 -> x0, starting transfers between devices: 3.97 us -> none  [on_device(): parts = lax.all_to_all(parts, 'gx', split_axis=0, concat_axis=0, tiled=True)]
    pallas_call x1, Pallas kernels: 16.2 us -> 12.5 us  [analyse(): pl.pallas_call(analysis_kernel, in_specs=[pl.BlockSpec(memory_space=pltpu...]
    pallas_call x4 -> x3, Pallas kernels: 8.07 us -> 5.04 us  [the longest x1 2.72 us: first_modes(): pl.pallas_call(first_kernel, in_specs=[SCALAR] + [WHOLE] * (GX + 1), out_...]
    all_to_all x1, waiting for transfers between devices: 1.85 us -> 3.52 us  [on_device(): even = lax.all_to_all(even, 'gy', split_axis=0, concat_axis=0, tiled=True)]
  transfers between devices with their start and end apart: 17 -> 16, of which waited for: 9 -> 8; matrix products, arithmetic and copies ran while one was open for 0% -> 0% of each run, Pallas kernels for 4% -> 4%
where the time goes in v1:
time: 107 us; the launch traced here: 106 us
  starting transfers between devices  39.8 us (37%)
  Pallas kernels  26.1 us (24%)
  blocking collectives  25 us (23%)
  waiting for transfers between devices  15.3 us (14%)
    ppermute x14, starting transfers between devices, shifted(): return lax.ppermute(block, 'gx', [(i, (i + shift) % GX) for i in range(GX)])  26.2 us
    all_to_all x1, blocking collectives, on_device(): parts = lax.all_to_all(parts, 'gy', split_axis=0, concat_axis=0, tiled=True)  15.5 us
    pallas_call x1, Pallas kernels, analyse(): pl.pallas_call(analysis_kernel, in_specs=[pl.BlockSpec(memory_space=pltpu...  12.5 us
    ppermute x14, waiting for transfers between devices, shifted(): return lax.ppermute(block, 'gx', [(i, (i + shift) % GX) for i in range(GX)])  11.1 us
    all_to_all x1, blocking collectives, on_device(): parts = lax.all_to_all(parts, 'gx', split_axis=0, concat_axis=0, tiled=True)  9.46 us
    pallas_call x1, Pallas kernels, depth_modes(): pl.pallas_call(depth_kernel, grid_spec=grid_spec, out_shape=[pltpu.HBM((G...  8.61 us
    all_to_all x1, starting transfers between devices, on_device(): cross = lax.all_to_all(cross, 'gy', split_axis=0, concat_axis=0, tiled=True)  7.13 us
    all_to_all x1, starting transfers between devices, on_device(): even = lax.all_to_all(even, 'gy', split_axis=0, concat_axis=0, tiled=True)  6.54 us
  transfers between devices with their start and end apart: 16, of which 8 were waited for; matrix products, arithmetic and copies ran while one was open for 0% of the time, Pallas kernels for 4%

profile of v1, /device:TPU:0, one launch (start us, length us, event | category | flops | bytes accessed | tf_op | source)
XLA Modules:
  0.0 106.3 jit_solution(8476894381561010493)
XLA Ops:
  0.0 8.6 %depth_modes.1 = (f32[16,16,16,128]{3,2,1,0:T(8,128)}, f32[8,128]{1,0:T(8,128)S(1)}, f32[520,128]{1,0:T(8,128)S(1)}, f32[520,128]{1,0:T(8,128)}, f32[520,128]{1,...) custom-call(s32[1]{0:T(128)} %bitcast.place, ...), custom_call_target="tpu_custom_call" | custom-call | tf_op jit(solution)/shard_map/depth_modes/pallas_call | solution.py:190
  8.6 7.1 %all-to-all-start.1 = ((f32[16,16,16,128]{3,2,1,0:T(8,128)}), f32[16,16,16,128]{3,2,1,0:T(8,128)S(1)}, u32[]{:S(2)}, u32[]{:S(2)}) async-start(f32[16,16,16,128]{3,2,1,0:T(8,128)} %get-tuple-element.32), calls=%async_computation.1 | async-start | bytes 4194304 | tf_op jit(solution)/shard_map/all_to_all | solution.py:467
  15.8 0.0 collective-permute-start
  15.8 2.0 %collective-permute-start.1 = (f32[520,128]{1,0:T(8,128)}, f32[520,128]{1,0:T(8,128)S(1)}, u32[]{:S(2)}, u32[]{:S(2)}) collective-permute-start(f32[520,128]{1,0:T(8,128)} %get-tuple-element.26), channel_id=1, source_target_pairs={{0,32},{16,48},{32,64},{48,80},{64,96},{80,112},{96,0},{112,16},{1... | collective-permute-start | bytes 798728 | tf_op jit(solution)/shard_map/ppermute | solution.py:450
  17.8 2.9 %collective-permute-start.2 = (f32[520,128]{1,0:T(8,128)}, f32[520,128]{1,0:T(8,128)S(1)}, u32[]{:S(2)}, u32[]{:S(2)}) collective-permute-start(f32[520,128]{1,0:T(8,128)} %get-tuple-element.27), channel_id=1, source_target_pairs={{0,48},{16,64},{32,80},{48,96},{64,112},{80,0},{96,16},{112,32},{1... | collective-permute-start | bytes 798728 | tf_op jit(solution)/shard_map/ppermute | solution.py:450
  20.7 1.2 %collective-permute-start.3 = (f32[520,128]{1,0:T(8,128)}, f32[520,128]{1,0:T(8,128)S(1)}, u32[]{:S(2)}, u32[]{:S(2)}) collective-permute-start(f32[520,128]{1,0:T(8,128)} %get-tuple-element.28), channel_id=1, source_target_pairs={{0,64},{16,80},{32,96},{48,112},{64,0},{80,16},{96,32},{112,48},{1... | collective-permute-start | bytes 798728 | tf_op jit(solution)/shard_map/ppermute | solution.py:450
  21.8 2.5 %collective-permute-start.4 = (f32[520,128]{1,0:T(8,128)}, f32[520,128]{1,0:T(8,128)S(1)}, u32[]{:S(2)}, u32[]{:S(2)}) collective-permute-start(f32[520,128]{1,0:T(8,128)} %get-tuple-element.29), channel_id=1, source_target_pairs={{0,80},{16,96},{32,112},{48,0},{64,16},{80,32},{96,48},{112,64},{1... | collective-permute-start | bytes 798728 | tf_op jit(solution)/shard_map/ppermute | solution.py:450
  24.3 0.6 collective-permute-done.refs_1_
  24.9 3.2 %collective-permute-start.5 = (f32[520,128]{1,0:T(8,128)}, f32[520,128]{1,0:T(8,128)S(1)}, u32[]{:S(2)}, u32[]{:S(2)}) collective-permute-start(f32[520,128]{1,0:T(8,128)} %get-tuple-element.30), channel_id=1, source_target_pairs={{0,96},{16,112},{32,0},{48,16},{64,32},{80,48},{96,64},{112,80},{1... | collective-permute-start | bytes 798728 | tf_op jit(solution)/shard_map/ppermute | solution.py:450
  28.1 0.0 collective-permute-done.1.refs_2_
  28.1 5.4 %collective-permute-start.6 = (f32[520,128]{1,0:T(8,128)}, f32[520,128]{1,0:T(8,128)S(1)}, u32[]{:S(2)}, u32[]{:S(2)}) collective-permute-start(f32[520,128]{1,0:T(8,128)} %get-tuple-element.31), channel_id=1, source_target_pairs={{0,112},{16,0},{32,16},{48,32},{64,48},{80,64},{96,80},{112,96},{1... | collective-permute-start | bytes 798728 | tf_op jit(solution)/shard_map/ppermute | solution.py:450
  33.5 5.4 %collective-permute-done.2.refs_3_ = f32[520,128]{1,0:T(8,128)S(1)} collective-permute-done((f32[520,128]{1,0:T(8,128)}, f32[520,128]{1,0:T(8,128)S(1)}, u32[]{:S(2)}, u32[]{:S(2)}) %collective-permute-start.2) | collective-permute-done | bytes 266272 | tf_op jit(solution)/shard_map/ppermute | solution.py:450
  39.0 1.2 %collective-permute-done.3.refs_4_ = f32[520,128]{1,0:T(8,128)S(1)} collective-permute-done((f32[520,128]{1,0:T(8,128)}, f32[520,128]{1,0:T(8,128)S(1)}, u32[]{:S(2)}, u32[]{:S(2)}) %collective-permute-start.3) | collective-permute-done | bytes 266272 | tf_op jit(solution)/shard_map/ppermute | solution.py:450
  40.2 1.2 %collective-permute-done.4.refs_5_ = f32[520,128]{1,0:T(8,128)S(1)} collective-permute-done((f32[520,128]{1,0:T(8,128)}, f32[520,128]{1,0:T(8,128)S(1)}, u32[]{:S(2)}, u32[]{:S(2)}) %collective-permute-start.4) | collective-permute-done | bytes 266272 | tf_op jit(solution)/shard_map/ppermute | solution.py:450
  41.4 0.7 collective-permute-done.5.refs_6_
  42.1 1.9 %collective-permute-done.6.refs_7_ = f32[520,128]{1,0:T(8,128)S(1)} collective-permute-done((f32[520,128]{1,0:T(8,128)}, f32[520,128]{1,0:T(8,128)S(1)}, u32[]{:S(2)}, u32[]{:S(2)}) %collective-permute-start.6) | collective-permute-done | bytes 266272 | tf_op jit(solution)/shard_map/ppermute | solution.py:450
  44.0 2.7 %first_modes.1 = f32[16,72,128]{2,1,0:T(8,128)} custom-call(s32[1]{0:T(128)} %bitcast.place, bf16[8,128,256]{2,1,0:T(8,128)(2,1)S(1)} %copy-done, f32[520,128]{1,0:T(8,128)S(1)} %get-tuple-element.24.refs_0_, f32[520,128]{1,0:T(8,128)S(1)} %collective-permute-done.refs_1_, f32[520,128]{1,0:T(8,128)S(1)} %collective-permute-done.1.refs_2_, ...), custom_call_target="tpu_custom_call" | custom-call | tf_op jit(solution)/shard_map/first_modes/pallas_call | solution.py:227
  46.8 0.7 all-to-all-done.1.cross
  47.4 6.5 %all-to-all-start = ((f32[16,72,128]{2,1,0:T(8,128)}), f32[16,72,128]{2,1,0:T(8,128)S(1)}, u32[]{:S(2)}, u32[]{:S(2)}) async-start(f32[16,72,128]{2,1,0:T(8,128)} %first_modes.1), calls=%async_computation | async-start | bytes 1179648 | tf_op jit(solution)/shard_map/all_to_all | solution.py:471
  54.0 1.3 %second_modes.1 = (f32[8,16,128]{2,1,0:T(8,128)S(1)}, f32[8,16,128]{2,1,0:T(8,128)}, f32[8,16,128]{2,1,0:T(8,128)}, f32[8,16,128]{2,1,0:T(8,128)}, f32[8,16,128]...) custom-call(s32[1]{0:T(128)} %bitcast.place, f32[2,128,256]{2,1,0:T(8,128)S(1)} %copy-done.1, ...), custom_call_target="tpu_custom_call" | custom-call | tf_op jit(solution)/shard_map/second_modes/pallas_call | solution.py:257
  55.3 0.8 collective-permute-start.7
  56.1 1.9 %collective-permute-start.8 = (f32[8,16,128]{2,1,0:T(8,128)}, f32[8,16,128]{2,1,0:T(8,128)S(1)}, u32[]{:S(2)}, u32[]{:S(2)}) collective-permute-start(f32[8,16,128]{2,1,0:T(8,128)} %get-tuple-element.35), channel_id=1, source_target_pairs={{0,32},{16,48},{32,64},{48,80},{64,96},{80,112},{96,0},{112,16},{1... | collective-permute-start | bytes 196616 | tf_op jit(solution)/shard_map/ppermute | solution.py:450
  58.0 0.2 collective-permute-start.9
  58.2 1.9 %collective-permute-start.10 = (f32[8,16,128]{2,1,0:T(8,128)}, f32[8,16,128]{2,1,0:T(8,128)S(1)}, u32[]{:S(2)}, u32[]{:S(2)}) collective-permute-start(f32[8,16,128]{2,1,0:T(8,128)} %get-tuple-element.37), channel_id=1, source_target_pairs={{0,64},{16,80},{32,96},{48,112},{64,0},{80,16},{96,32},{112,48},{1... | collective-permute-start | bytes 196616 | tf_op jit(solution)/shard_map/ppermute | solution.py:450
  60.1 2.8 %collective-permute-start.11 = (f32[8,16,128]{2,1,0:T(8,128)}, f32[8,16,128]{2,1,0:T(8,128)S(1)}, u32[]{:S(2)}, u32[]{:S(2)}) collective-permute-start(f32[8,16,128]{2,1,0:T(8,128)} %get-tuple-element.38), channel_id=1, source_target_pairs={{0,80},{16,96},{32,112},{48,0},{64,16},{80,32},{96,48},{112,64},{1... | collective-permute-start | bytes 196616 | tf_op jit(solution)/shard_map/ppermute | solution.py:450
  62.9 1.4 %collective-permute-start.12 = (f32[8,16,128]{2,1,0:T(8,128)}, f32[8,16,128]{2,1,0:T(8,128)S(1)}, u32[]{:S(2)}, u32[]{:S(2)}) collective-permute-start(f32[8,16,128]{2,1,0:T(8,128)} %get-tuple-element.39), channel_id=1, source_target_pairs={{0,96},{16,112},{32,0},{48,16},{64,32},{80,48},{96,64},{112,80},{1... | collective-permute-start | bytes 196616 | tf_op jit(solution)/shard_map/ppermute | solution.py:450
  64.3 0.0 collective-permute-start.13
  64.3 3.5 %all-to-all-done.even_ref = f32[16,72,128]{2,1,0:T(8,128)S(1)} async-done(((f32[16,72,128]{2,1,0:T(8,128)}), f32[16,72,128]{2,1,0:T(8,128)S(1)}, u32[]{:S(2)}, u32[]{:S(2)}) %all-to-all-start) | async-done | bytes 589856 | tf_op jit(solution)/shard_map/all_to_all | solution.py:471
  67.8 1.0 gram.1
  68.8 9.5 %all_to_all.20 = f32[8,32,128]{2,1,0:T(8,128)S(1)} all-to-all(f32[8,32,128]{2,1,0:T(8,128)S(1)} %gram.1), channel_id=1, replica_groups=mesh['gx'=8,'gy'=16] {'gx'}, dimensions={0} | all-to-all | bytes 262144 | tf_op jit(solution)/shard_map/all_to_all | solution.py:474
  78.3 15.5 %all_to_all.21.parts = f32[16,32,128]{2,1,0:T(8,128)S(1)} all-to-all(f32[16,32,128]{2,1,0:T(8,128)S(1)} %broadcast_in_dim.3), channel_id=1, replica_groups=mesh['gx'=8,'gy'=16] {'gy'}, dimensions={0} | all-to-all | bytes 524288 | tf_op jit(solution)/shard_map/all_to_all | solution.py:476
  93.9 12.5 %analysis.1 = f32[64,32,1024]{2,1,0:T(8,128)} custom-call(f32[16,32,128]{2,1,0:T(8,128)S(1)} %all_to_all.21.parts, s32[1,64]{1,0:T(1,128)S(1)} %bitcast.4, f32[64,32,1024]{2,1,0:T(8,128)} %ens_hbm.1), custom_call_target="tpu_custom_call" | custom-call | tf_op jit(solution)/shard_map/analysis/pallas_call | solution.py:427
  (15 shorter events, 0.1 us)
Async XLA Ops:
  0.0 44.0 %copy-start = (bf16[8,128,256]{2,1,0:T(8,128)(2,1)S(1)}, bf16[8,128,256]{2,1,0:T(8,128)(2,1)}, u32[]{:S(2)}) copy-start(bf16[8,128,256]{2,1,0:T(8,128)(2,1)} %constant.14.clone.table_ref.first_table) | copy-start | bytes 1572868
  0.0 54.0 %copy-start.1 = (f32[2,128,256]{2,1,0:T(8,128)S(1)}, f32[2,128,256]{2,1,0:T(8,128)}, u32[]{:S(2)}) copy-start(f32[2,128,256]{2,1,0:T(8,128)} %constant.15.clone.table_ref) | copy-start | bytes 786436
  8.6 85.2 %copy-start.2 = (s32[64]{0:T(128)S(1)}, s32[64]{0:T(128)}, u32[]{:S(2)}) copy-start(s32[64]{0:T(128)} %param.10) | copy-start | bytes 772
  8.6 38.8 %all-to-all-start.1 = ((f32[16,16,16,128]{3,2,1,0:T(8,128)}), f32[16,16,16,128]{3,2,1,0:T(8,128)S(1)}, u32[]{:S(2)}, u32[]{:S(2)}) async-start(f32[16,16,16,128]{3,2,1,0:T(8,128)} %get-tuple-element.32), calls=%async_computation.1 | async-start | bytes 4194304 | tf_op jit(solution)/shard_map/all_to_all | solution.py:467
  15.8 9.1 %collective-permute-start = (f32[520,128]{1,0:T(8,128)}, f32[520,128]{1,0:T(8,128)S(1)}, u32[]{:S(2)}, u32[]{:S(2)}) collective-permute-start(f32[520,128]{1,0:T(8,128)} %get-tuple-element.25), channel_id=1, source_target_pairs={{0,16},{16,32},{32,48},{48,64},{64,80},{80,96},{96,112},{112,0},{1... | collective-permute-start | bytes 798728 | tf_op jit(solution)/shard_map/ppermute | solution.py:450
  15.8 12.3 %collective-permute-start.1 = (f32[520,128]{1,0:T(8,128)}, f32[520,128]{1,0:T(8,128)S(1)}, u32[]{:S(2)}, u32[]{:S(2)}) collective-permute-start(f32[520,128]{1,0:T(8,128)} %get-tuple-element.26), channel_id=1, source_target_pairs={{0,32},{16,48},{32,64},{48,80},{64,96},{80,112},{96,0},{112,16},{1... | collective-permute-start | bytes 798728 | tf_op jit(solution)/shard_map/ppermute | solution.py:450
  17.8 21.2 %collective-permute-start.2 = (f32[520,128]{1,0:T(8,128)}, f32[520,128]{1,0:T(8,128)S(1)}, u32[]{:S(2)}, u32[]{:S(2)}) collective-permute-start(f32[520,128]{1,0:T(8,128)} %get-tuple-element.27), channel_id=1, source_target_pairs={{0,48},{16,64},{32,80},{48,96},{64,112},{80,0},{96,16},{112,32},{1... | collective-permute-start | bytes 798728 | tf_op jit(solution)/shard_map/ppermute | solution.py:450
  20.7 19.5 %collective-permute-start.3 = (f32[520,128]{1,0:T(8,128)}, f32[520,128]{1,0:T(8,128)S(1)}, u32[]{:S(2)}, u32[]{:S(2)}) collective-permute-start(f32[520,128]{1,0:T(8,128)} %get-tuple-element.28), channel_id=1, source_target_pairs={{0,64},{16,80},{32,96},{48,112},{64,0},{80,16},{96,32},{112,48},{1... | collective-permute-start | bytes 798728 | tf_op jit(solution)/shard_map/ppermute | solution.py:450
  21.8 19.5 %collective-permute-start.4 = (f32[520,128]{1,0:T(8,128)}, f32[520,128]{1,0:T(8,128)S(1)}, u32[]{:S(2)}, u32[]{:S(2)}) collective-permute-start(f32[520,128]{1,0:T(8,128)} %get-tuple-element.29), channel_id=1, source_target_pairs={{0,80},{16,96},{32,112},{48,0},{64,16},{80,32},{96,48},{112,64},{1... | collective-permute-start | bytes 798728 | tf_op jit(solution)/shard_map/ppermute | solution.py:450
  24.9 17.2 %collective-permute-start.5 = (f32[520,128]{1,0:T(8,128)}, f32[520,128]{1,0:T(8,128)S(1)}, u32[]{:S(2)}, u32[]{:S(2)}) collective-permute-start(f32[520,128]{1,0:T(8,128)} %get-tuple-element.30), channel_id=1, source_target_pairs={{0,96},{16,112},{32,0},{48,16},{64,32},{80,48},{96,64},{112,80},{1... | collective-permute-start | bytes 798728 | tf_op jit(solution)/shard_map/ppermute | solution.py:450
  28.1 15.9 %collective-permute-start.6 = (f32[520,128]{1,0:T(8,128)}, f32[520,128]{1,0:T(8,128)S(1)}, u32[]{:S(2)}, u32[]{:S(2)}) collective-permute-start(f32[520,128]{1,0:T(8,128)} %get-tuple-element.31), channel_id=1, source_target_pairs={{0,112},{16,0},{32,16},{48,32},{64,48},{80,64},{96,80},{112,96},{1... | collective-permute-start | bytes 798728 | tf_op jit(solution)/shard_map/ppermute | solution.py:450
  47.4 20.4 %all-to-all-start = ((f32[16,72,128]{2,1,0:T(8,128)}), f32[16,72,128]{2,1,0:T(8,128)S(1)}, u32[]{:S(2)}, u32[]{:S(2)}) async-start(f32[16,72,128]{2,1,0:T(8,128)} %first_modes.1), calls=%async_computation | async-start | bytes 1179648 | tf_op jit(solution)/shard_map/all_to_all | solution.py:471
  55.3 7.6 %collective-permute-start.7 = (f32[8,16,128]{2,1,0:T(8,128)}, f32[8,16,128]{2,1,0:T(8,128)S(1)}, u32[]{:S(2)}, u32[]{:S(2)}) collective-permute-start(f32[8,16,128]{2,1,0:T(8,128)} %get-tuple-element.34), channel_id=1, source_target_pairs={{0,16},{16,32},{32,48},{48,64},{64,80},{80,96},{96,112},{112,0},{1... | collective-permute-start | bytes 196616 | tf_op jit(solution)/shard_map/ppermute | solution.py:450
  56.1 8.2 %collective-permute-start.8 = (f32[8,16,128]{2,1,0:T(8,128)}, f32[8,16,128]{2,1,0:T(8,128)S(1)}, u32[]{:S(2)}, u32[]{:S(2)}) collective-permute-start(f32[8,16,128]{2,1,0:T(8,128)} %get-tuple-element.35), channel_id=1, source_target_pairs={{0,32},{16,48},{32,64},{48,80},{64,96},{80,112},{96,0},{112,16},{1... | collective-permute-start | bytes 196616 | tf_op jit(solution)/shard_map/ppermute | solution.py:450
  58.0 9.8 %collective-permute-start.9 = (f32[8,16,128]{2,1,0:T(8,128)}, f32[8,16,128]{2,1,0:T(8,128)S(1)}, u32[]{:S(2)}, u32[]{:S(2)}) collective-permute-start(f32[8,16,128]{2,1,0:T(8,128)} %get-tuple-element.36), channel_id=1, source_target_pairs={{0,48},{16,64},{32,80},{48,96},{64,112},{80,0},{96,16},{112,32},{1... | collective-permute-start | bytes 196616 | tf_op jit(solution)/shard_map/ppermute | solution.py:450
  58.2 9.6 %collective-permute-start.10 = (f32[8,16,128]{2,1,0:T(8,128)}, f32[8,16,128]{2,1,0:T(8,128)S(1)}, u32[]{:S(2)}, u32[]{:S(2)}) collective-permute-start(f32[8,16,128]{2,1,0:T(8,128)} %get-tuple-element.37), channel_id=1, source_target_pairs={{0,64},{16,80},{32,96},{48,112},{64,0},{80,16},{96,32},{112,48},{1... | collective-permute-start | bytes 196616 | tf_op jit(solution)/shard_map/ppermute | solution.py:450
  60.1 7.7 %collective-permute-start.11 = (f32[8,16,128]{2,1,0:T(8,128)}, f32[8,16,128]{2,1,0:T(8,128)S(1)}, u32[]{:S(2)}, u32[]{:S(2)}) collective-permute-start(f32[8,16,128]{2,1,0:T(8,128)} %get-tuple-element.38), channel_id=1, source_target_pairs={{0,80},{16,96},{32,112},{48,0},{64,16},{80,32},{96,48},{112,64},{1... | collective-permute-start | bytes 196616 | tf_op jit(solution)/shard_map/ppermute | solution.py:450
  62.9 4.9 %collective-permute-start.12 = (f32[8,16,128]{2,1,0:T(8,128)}, f32[8,16,128]{2,1,0:T(8,128)S(1)}, u32[]{:S(2)}, u32[]{:S(2)}) collective-permute-start(f32[8,16,128]{2,1,0:T(8,128)} %get-tuple-element.39), channel_id=1, source_target_pairs={{0,96},{16,112},{32,0},{48,16},{64,32},{80,48},{96,64},{112,80},{1... | collective-permute-start | bytes 196616 | tf_op jit(solution)/shard_map/ppermute | solution.py:450
  64.3 3.5 %collective-permute-start.13 = (f32[8,16,128]{2,1,0:T(8,128)}, f32[8,16,128]{2,1,0:T(8,128)S(1)}, u32[]{:S(2)}, u32[]{:S(2)}) collective-permute-start(f32[8,16,128]{2,1,0:T(8,128)} %get-tuple-element.40), channel_id=1, source_target_pairs={{0,112},{16,0},{32,16},{48,32},{64,48},{80,64},{96,80},{112,96},{1... | collective-permute-start | bytes 196616 | tf_op jit(solution)/shard_map/ppermute | solution.py:450

commit v2 on v1

--- a/solution.py
+++ b/solution.py
@@ -50,7 +50,7 @@
         for y4 in range(4):
             cols = slice(64 * y4, 64 * y4 + 64)
             for h in range(GY):
-                out[g, 16 * y4 + h, cols] = bz[2 * h + 1]
+                out[g, 16 * y4 + h, cols] = bz[2 * (GY - 1 - h) + 1]
             for s in range(GX):
                 for c2 in range(2):
                     out[g, 64 + 8 * s + 2 * y4 + c2, cols] = bz[4 * ((g + s) % GX) + 2 * c2]
@@ -59,13 +59,13 @@
 
 def first_tables():
     bx = basis(NX, XM)
-    out = np.zeros((GX, XM, 2, GX, LX // 2))
+    out = np.zeros((GX, XM, GX, 2, LX // 2))
     for g in range(GX):
         for s in range(GX):
             start = LX * ((g - s) % GX)
             block = bx[:, start : start + LX]
-            out[g, :, 0, s, :] = block[:, 0::2]
-            out[g, :, 1, s, :] = block[:, 1::2]
+            out[g, :, s, 0, :] = block[:, 0::2]
+            out[g, :, s, 1, :] = block[:, 1::2]
     return two_parts(out.reshape(GX, XM, NX), 1)
 
 
@@ -198,7 +198,24 @@
     )(place, ensemble, tables, index, scale)
 
 
-def first_kernel(place, table_ref, *refs):
+def first_product(blocks, columns, table, y):
+    value = [
+        jnp.concatenate(
+            [unpair(*[b[pl.ds(2 * k + c2, 16, stride=32), :] for c2 in range(2)]) for b in blocks]
+        )
+        for k in (y, y + 1)
+    ]
+    return contract(table[:, columns], jnp.concatenate(value, axis=1))
+
+
+def first_half_kernel(place, table_ref, *refs):
+    blocks, out = refs[: GX // 2], refs[GX // 2]
+    table = table_ref[place[0]]
+    for y in range(0, LY, 2):
+        out[y // 2] = first_product(blocks, slice(0, NX // 2), table, y)
+
+
+def first_kernel(place, table_ref, half, *refs):
     blocks, out_ref, held = refs[:GX], refs[GX], refs[GX + 1]
     out = out_ref.reshape(XM * 18, 128)
     held[64:, :] = jnp.zeros((64, 128), f32)
@@ -209,30 +226,30 @@
     out[pl.ds(17, XM, stride=18), :] = jnp.zeros((XM, 128), f32)
     table = table_ref[place[0]]
     for y in range(0, LY, 2):
-        value = [
-            unpair(
-                *[
-                    jnp.concatenate([b[pl.ds(2 * k + c2, 16, stride=32), :] for b in blocks])
-                    for c2 in range(2)
-                ]
-            )
-            for k in (y, y + 1)
-        ]
-        modes = contract(table, jnp.concatenate(value, axis=1))
+        modes = half[y // 2] + first_product(blocks[GX // 2 :], slice(NX // 2, NX), table, y)
         for k in range(2):
             out[pl.ds(y + k, XM, stride=18), :] = modes[:, 128 * k : 128 * k + 128]
 
 
 def first_modes(place, tables, blocks):
+    params = pltpu.CompilerParams(vmem_limit_bytes=16 << 20)
+    half = pl.pallas_call(
+        first_half_kernel,
+        in_specs=[SCALAR] + [WHOLE] * (GX // 2 + 1),
+        out_specs=WHOLE,
+        out_shape=jax.ShapeDtypeStruct((LY // 2, XM, 256), f32),
+        compiler_params=params,
+        name="first_half",
+    )(place, tables, *blocks[: GX // 2])
     return pl.pallas_call(
         first_kernel,
-        in_specs=[SCALAR] + [WHOLE] * (GX + 1),
+        in_specs=[SCALAR] + [WHOLE] * (GX + 2),
         out_specs=WHOLE,
         out_shape=pltpu.HBM((GY, 72, 128), f32),
         scratch_shapes=[pltpu.VMEM((128, 128), f32)],
-        compiler_params=pltpu.CompilerParams(vmem_limit_bytes=16 << 20),
+        compiler_params=params,
         name="first_modes",
-    )(place, tables, *blocks)
+    )(place, tables, half, *blocks)
 
 
 def second_kernel(place, table_ref, cross, *outs):
@@ -240,7 +257,7 @@
     for group in range(LX // 4):
         value = jnp.concatenate(
             [
-                jnp.concatenate([cross[h, 2 * group + pair] for h in range(GY)])
+                jnp.concatenate([cross[h, 2 * group + pair] for h in reversed(range(GY))])
                 for pair in range(2)
             ],
             axis=1,
@@ -297,7 +314,7 @@
     rows = []
     for b in range(0, 8, 4):
         value = [
-            unpair(*[jnp.concatenate([ref[k + b2] for ref in odd_refs]) for b2 in range(2)])
+            jnp.concatenate([unpair(*[ref[k + b2] for b2 in range(2)]) for ref in odd_refs])
             for k in (b, b + 2)
         ]
         modes = contract(table, jnp.concatenate(value, axis=1))
@@ -450,6 +467,13 @@
     return lax.ppermute(block, "gx", [(i, (i + shift) % GX) for i in range(GX)])
 
 
+def backwards(blocks, axis):
+    order = [list(range(blocks.shape[0]))[::-1]]
+    return lax.all_to_all(
+        blocks, axis, split_axis=0, concat_axis=0, tiled=True, axis_index_groups=order
+    )
+
+
 def on_device(ensemble, obs_index, obs_scale, member_order):
     gx = lax.axis_index("gx")
     place = gx.astype(jnp.int32).reshape(1)
@@ -464,16 +488,16 @@
         in_hbm(obs_index.reshape(OBS_DEV // 128, 128)),
         in_hbm(obs_scale.reshape(OBS_DEV // 128, 128)),
     )
-    cross = lax.all_to_all(cross, "gy", split_axis=0, concat_axis=0, tiled=True)
+    cross = backwards(cross, "gy")
     rows = [rows[0]] + [shifted(rows[s], s) for s in range(1, GX)]
     even = first_modes(place, first_table, rows)
     odd = second_modes(place, y_table, cross)
     even = lax.all_to_all(even, "gy", split_axis=0, concat_axis=0, tiled=True)
     odd = [odd[0]] + [shifted(odd[s], s) for s in range(1, GX)]
     parts = gram(place, first_table, y_table, odd_weight, even, odd)
-    parts = lax.all_to_all(parts, "gx", split_axis=0, concat_axis=0, tiled=True)
+    parts = backwards(parts, "gx")
     parts = jnp.broadcast_to(jnp.sum(parts, axis=0), (GY, 32, 128))
-    parts = lax.all_to_all(parts, "gy", split_axis=0, concat_axis=0, tiled=True)
+    parts = backwards(parts, "gy")
     return analyse(parts, member_order.reshape(1, M), ensemble)
 
 

time: 107 us -> 102 us (0.953)
  blocking collectives: 25 us -> 22.4 us
  waiting for transfers between devices: 15.3 us -> 13.6 us
    all_to_all x2, blocking collectives: 25 us -> 22.4 us  [backwards(): lax.all_to_all(blocks, axis, split_axis=0, concat_axis=0, tiled=True, axi...]
    all_to_all x1, starting transfers between devices: 6.54 us -> 4.13 us  [on_device(): even = lax.all_to_all(even, 'gy', split_axis=0, concat_axis=0, tiled=True)]
    all_to_all x1, starting transfers between devices: 7.13 us -> 8.9 us  [backwards(): lax.all_to_all(blocks, axis, split_axis=0, concat_axis=0, tiled=True, axi...]
    all_to_all x1, waiting for transfers between devices: 3.52 us -> 2.29 us  [on_device(): even = lax.all_to_all(even, 'gy', split_axis=0, concat_axis=0, tiled=True)]
    pallas_call x1 -> x2, Pallas kernels: 2.72 us -> 2.79 us  [the longest x1 1.82 us: first_modes(): pl.pallas_call(first_kernel, in_specs=[SCALAR] + [WHOLE] * (GX + 2), out_...]
where the time goes in v2:
time: 102 us
  starting transfers between devices  39.7 us (39%)
  Pallas kernels  26.2 us (26%)
  blocking collectives  22.4 us (22%)
  waiting for transfers between devices  13.6 us (13%)
    ppermute x14, starting transfers between devices, shifted(): return lax.ppermute(block, 'gx', [(i, (i + shift) % GX) for i in range(GX)])  26.7 us
    all_to_all x2, blocking collectives, backwards(): lax.all_to_all(blocks, axis, split_axis=0, concat_axis=0, tiled=True, axi...  22.4 us
    pallas_call x1, Pallas kernels, analyse(): pl.pallas_call(analysis_kernel, in_specs=[pl.BlockSpec(memory_space=pltpu...  12.5 us
    ppermute x14, waiting for transfers between devices, shifted(): return lax.ppermute(block, 'gx', [(i, (i + shift) % GX) for i in range(GX)])  11.3 us
    all_to_all x1, starting transfers between devices, backwards(): lax.all_to_all(blocks, axis, split_axis=0, concat_axis=0, tiled=True, axi...  8.9 us
    pallas_call x1, Pallas kernels, depth_modes(): pl.pallas_call(depth_kernel, grid_spec=grid_spec, out_shape=[pltpu.HBM((G...  8.61 us
    all_to_all x1, starting transfers between devices, on_device(): even = lax.all_to_all(even, 'gy', split_axis=0, concat_axis=0, tiled=True)  4.13 us
    all_to_all x1, waiting for transfers between devices, on_device(): even = lax.all_to_all(even, 'gy', split_axis=0, concat_axis=0, tiled=True)  2.29 us
  transfers between devices with their start and end apart: 16, of which 8 were waited for; matrix products, arithmetic and copies ran while one was open for 0% of the time, Pallas kernels for 4%

profile of v2, /device:TPU:0, one launch (start us, length us, event | category | flops | bytes accessed | tf_op | source)
XLA Modules:
  0.0 102.0 jit_solution(10278548582179397512)
XLA Ops:
  0.0 8.6 %depth_modes.1 = (f32[16,16,16,128]{3,2,1,0:T(8,128)}, f32[8,128]{1,0:T(8,128)S(1)}, f32[520,128]{1,0:T(8,128)S(1)}, f32[520,128]{1,0:T(8,128)}, f32[520,128]{1,...) custom-call(s32[1]{0:T(128)} %bitcast.place, ...), custom_call_target="tpu_custom_call" | custom-call | tf_op jit(solution)/shard_map/depth_modes/pallas_call | solution.py:190
  8.6 8.9 %all-to-all-start.1 = ((f32[16,16,16,128]{3,2,1,0:T(8,128)}), f32[16,16,16,128]{3,2,1,0:T(8,128)S(1)}, u32[]{:S(2)}, u32[]{:S(2)}) async-start(f32[16,16,16,128]{3,2,1,0:T(8,128)} %get-tuple-element.32), calls=%async_computation.1 | async-start | bytes 4194304 | tf_op jit(solution)/shard_map/all_to_all | solution.py:472
  17.5 2.0 %collective-permute-start.1 = (f32[520,128]{1,0:T(8,128)}, f32[520,128]{1,0:T(8,128)S(1)}, u32[]{:S(2)}, u32[]{:S(2)}) collective-permute-start(f32[520,128]{1,0:T(8,128)} %get-tuple-element.26), channel_id=1, source_target_pairs={{0,32},{16,48},{32,64},{48,80},{64,96},{80,112},{96,0},{112,16},{1... | collective-permute-start | bytes 798728 | tf_op jit(solution)/shard_map/ppermute | solution.py:467
  19.5 2.9 %collective-permute-start.2 = (f32[520,128]{1,0:T(8,128)}, f32[520,128]{1,0:T(8,128)S(1)}, u32[]{:S(2)}, u32[]{:S(2)}) collective-permute-start(f32[520,128]{1,0:T(8,128)} %get-tuple-element.27), channel_id=1, source_target_pairs={{0,48},{16,64},{32,80},{48,96},{64,112},{80,0},{96,16},{112,32},{1... | collective-permute-start | bytes 798728 | tf_op jit(solution)/shard_map/ppermute | solution.py:467
  22.4 1.2 %collective-permute-start.3 = (f32[520,128]{1,0:T(8,128)}, f32[520,128]{1,0:T(8,128)S(1)}, u32[]{:S(2)}, u32[]{:S(2)}) collective-permute-start(f32[520,128]{1,0:T(8,128)} %get-tuple-element.28), channel_id=1, source_target_pairs={{0,64},{16,80},{32,96},{48,112},{64,0},{80,16},{96,32},{112,48},{1... | collective-permute-start | bytes 798728 | tf_op jit(solution)/shard_map/ppermute | solution.py:467
  23.6 2.5 %collective-permute-start.4 = (f32[520,128]{1,0:T(8,128)}, f32[520,128]{1,0:T(8,128)S(1)}, u32[]{:S(2)}, u32[]{:S(2)}) collective-permute-start(f32[520,128]{1,0:T(8,128)} %get-tuple-element.29), channel_id=1, source_target_pairs={{0,80},{16,96},{32,112},{48,0},{64,16},{80,32},{96,48},{112,64},{1... | collective-permute-start | bytes 798728 | tf_op jit(solution)/shard_map/ppermute | solution.py:467
  26.1 0.6 collective-permute-done.refs_1_
  26.6 3.2 %collective-permute-start.5 = (f32[520,128]{1,0:T(8,128)}, f32[520,128]{1,0:T(8,128)S(1)}, u32[]{:S(2)}, u32[]{:S(2)}) collective-permute-start(f32[520,128]{1,0:T(8,128)} %get-tuple-element.30), channel_id=1, source_target_pairs={{0,96},{16,112},{32,0},{48,16},{64,32},{80,48},{96,64},{112,80},{1... | collective-permute-start | bytes 798728 | tf_op jit(solution)/shard_map/ppermute | solution.py:467
  29.9 0.0 collective-permute-done.1.refs_2_
  29.9 5.4 %collective-permute-start.6 = (f32[520,128]{1,0:T(8,128)}, f32[520,128]{1,0:T(8,128)S(1)}, u32[]{:S(2)}, u32[]{:S(2)}) collective-permute-start(f32[520,128]{1,0:T(8,128)} %get-tuple-element.31), channel_id=1, source_target_pairs={{0,112},{16,0},{32,16},{48,32},{64,48},{80,64},{96,80},{112,96},{1... | collective-permute-start | bytes 798728 | tf_op jit(solution)/shard_map/ppermute | solution.py:467
  35.3 5.4 %collective-permute-done.2.refs_3_ = f32[520,128]{1,0:T(8,128)S(1)} collective-permute-done((f32[520,128]{1,0:T(8,128)}, f32[520,128]{1,0:T(8,128)S(1)}, u32[]{:S(2)}, u32[]{:S(2)}) %collective-permute-start.2) | collective-permute-done | bytes 266272 | tf_op jit(solution)/shard_map/ppermute | solution.py:467
  40.7 1.0 first_half.1.half
  41.7 0.2 collective-permute-done.3.refs_4_
  41.9 1.2 %collective-permute-done.4.refs_5_ = f32[520,128]{1,0:T(8,128)S(1)} collective-permute-done((f32[520,128]{1,0:T(8,128)}, f32[520,128]{1,0:T(8,128)S(1)}, u32[]{:S(2)}, u32[]{:S(2)}) %collective-permute-start.4) | collective-permute-done | bytes 266272 | tf_op jit(solution)/shard_map/ppermute | solution.py:467
  43.1 0.7 collective-permute-done.5.refs_6_
  43.9 1.9 %collective-permute-done.6.refs_7_ = f32[520,128]{1,0:T(8,128)S(1)} collective-permute-done((f32[520,128]{1,0:T(8,128)}, f32[520,128]{1,0:T(8,128)S(1)}, u32[]{:S(2)}, u32[]{:S(2)}) %collective-permute-start.6) | collective-permute-done | bytes 266272 | tf_op jit(solution)/shard_map/ppermute | solution.py:467
  45.8 1.8 %first_modes.1 = f32[16,72,128]{2,1,0:T(8,128)} custom-call(s32[1]{0:T(128)} %bitcast.place, bf16[8,128,256]{2,1,0:T(8,128)(2,1)S(1)} %copy-done, f32[8,64,256]{2,1,0:T(8,128)S(1)} %first_half.1.half, f32[520,128]{1,0:T(8,128)S(1)} %get-tuple-element.24.refs_0_, f32[520,128]{1,0:T(8,128)S(1)} %collective-permute-done.refs_1_, ...), custom_call_target="tpu_custom_call" | custom-call | tf_op jit(solution)/shard_map/first_modes/pallas_call | solution.py:244
  47.6 4.1 %all-to-all-start = ((f32[16,72,128]{2,1,0:T(8,128)}), f32[16,72,128]{2,1,0:T(8,128)S(1)}, u32[]{:S(2)}, u32[]{:S(2)}) async-start(f32[16,72,128]{2,1,0:T(8,128)} %first_modes.1), calls=%async_computation | async-start | bytes 1179648 | tf_op jit(solution)/shard_map/all_to_all | solution.py:495
  51.8 1.3 %second_modes.1 = (f32[8,16,128]{2,1,0:T(8,128)S(1)}, f32[8,16,128]{2,1,0:T(8,128)}, f32[8,16,128]{2,1,0:T(8,128)}, f32[8,16,128]{2,1,0:T(8,128)}, f32[8,16,128]...) custom-call(s32[1]{0:T(128)} %bitcast.place, f32[2,128,256]{2,1,0:T(8,128)S(1)} %copy-done.1, ...), custom_call_target="tpu_custom_call" | custom-call | tf_op jit(solution)/shard_map/second_modes/pallas_call | solution.py:274
  53.1 0.5 collective-permute-start.7
  53.6 1.9 %collective-permute-start.8 = (f32[8,16,128]{2,1,0:T(8,128)}, f32[8,16,128]{2,1,0:T(8,128)S(1)}, u32[]{:S(2)}, u32[]{:S(2)}) collective-permute-start(f32[8,16,128]{2,1,0:T(8,128)} %get-tuple-element.35), channel_id=1, source_target_pairs={{0,32},{16,48},{32,64},{48,80},{64,96},{80,112},{96,0},{112,16},{1... | collective-permute-start | bytes 196616 | tf_op jit(solution)/shard_map/ppermute | solution.py:467
  55.5 2.4 %collective-permute-start.9 = (f32[8,16,128]{2,1,0:T(8,128)}, f32[8,16,128]{2,1,0:T(8,128)S(1)}, u32[]{:S(2)}, u32[]{:S(2)}) collective-permute-start(f32[8,16,128]{2,1,0:T(8,128)} %get-tuple-element.36), channel_id=1, source_target_pairs={{0,48},{16,64},{32,80},{48,96},{64,112},{80,0},{96,16},{112,32},{1... | collective-permute-start | bytes 196616 | tf_op jit(solution)/shard_map/ppermute | solution.py:467
  58.0 1.2 %collective-permute-start.10 = (f32[8,16,128]{2,1,0:T(8,128)}, f32[8,16,128]{2,1,0:T(8,128)S(1)}, u32[]{:S(2)}, u32[]{:S(2)}) collective-permute-start(f32[8,16,128]{2,1,0:T(8,128)} %get-tuple-element.37), channel_id=1, source_target_pairs={{0,64},{16,80},{32,96},{48,112},{64,0},{80,16},{96,32},{112,48},{1... | collective-permute-start | bytes 196616 | tf_op jit(solution)/shard_map/ppermute | solution.py:467
  59.1 2.4 %collective-permute-start.11 = (f32[8,16,128]{2,1,0:T(8,128)}, f32[8,16,128]{2,1,0:T(8,128)S(1)}, u32[]{:S(2)}, u32[]{:S(2)}) collective-permute-start(f32[8,16,128]{2,1,0:T(8,128)} %get-tuple-element.38), channel_id=1, source_target_pairs={{0,80},{16,96},{32,112},{48,0},{64,16},{80,32},{96,48},{112,64},{1... | collective-permute-start | bytes 196616 | tf_op jit(solution)/shard_map/ppermute | solution.py:467
  61.6 0.0 collective-permute-done.7.refs_1_
  61.6 1.0 collective-permute-start.12
  62.6 2.3 %all-to-all-done.even_ref = f32[16,72,128]{2,1,0:T(8,128)S(1)} async-done(((f32[16,72,128]{2,1,0:T(8,128)}), f32[16,72,128]{2,1,0:T(8,128)S(1)}, u32[]{:S(2)}, u32[]{:S(2)}) %all-to-all-start) | async-done | bytes 589856 | tf_op jit(solution)/shard_map/all_to_all | solution.py:495
  64.9 1.2 %collective-permute-done.12.refs_6_ = f32[8,16,128]{2,1,0:T(8,128)S(1)} collective-permute-done((f32[8,16,128]{2,1,0:T(8,128)}, f32[8,16,128]{2,1,0:T(8,128)S(1)}, u32[]{:S(2)}, u32[]{:S(2)}) %collective-permute-start.12) | collective-permute-done | bytes 65568 | tf_op jit(solution)/shard_map/ppermute | solution.py:467
  66.1 1.0 gram.1
  67.1 9.0 %all_to_all.20 = f32[8,32,128]{2,1,0:T(8,128)S(1)} all-to-all(f32[8,32,128]{2,1,0:T(8,128)S(1)} %gram.1), channel_id=1, replica_groups={{112,96,80,64,48,32,16,0},{113,97,81,65,49,33,17,1},{114,98,82,66,50,34..., dimensions={0} | all-to-all | bytes 262144 | tf_op jit(solution)/shard_map/all_to_all | solution.py:472
  76.1 13.4 %all_to_all.21.parts = f32[16,32,128]{2,1,0:T(8,128)S(1)} all-to-all(f32[16,32,128]{2,1,0:T(8,128)S(1)} %broadcast_in_dim.3), channel_id=1, replica_groups={{15,14,13,12,11,10,9,8,7,6,5,4,3,2,1,0},{31,30,29,28,27,26,25,24,23,22,..., dimensions={0} | all-to-all | bytes 524288 | tf_op jit(solution)/shard_map/all_to_all | solution.py:472
  89.6 12.5 %analysis.1 = f32[64,32,1024]{2,1,0:T(8,128)} custom-call(f32[16,32,128]{2,1,0:T(8,128)S(1)} %all_to_all.21.parts, s32[1,64]{1,0:T(1,128)S(1)} %bitcast.4, f32[64,32,1024]{2,1,0:T(8,128)} %ens_hbm.1), custom_call_target="tpu_custom_call" | custom-call | tf_op jit(solution)/shard_map/analysis/pallas_call | solution.py:444
  (16 shorter events, 0.1 us)
Async XLA Ops:
  0.0 40.7 %copy-start = (bf16[8,128,256]{2,1,0:T(8,128)(2,1)S(1)}, bf16[8,128,256]{2,1,0:T(8,128)(2,1)}, u32[]{:S(2)}) copy-start(bf16[8,128,256]{2,1,0:T(8,128)(2,1)} %constant.14.clone.table_ref.first_table) | copy-start | bytes 1572868
  0.0 51.7 %copy-start.1 = (f32[2,128,256]{2,1,0:T(8,128)S(1)}, f32[2,128,256]{2,1,0:T(8,128)}, u32[]{:S(2)}) copy-start(f32[2,128,256]{2,1,0:T(8,128)} %constant.15.clone.table_ref) | copy-start | bytes 786436
  8.6 80.9 %copy-start.2 = (s32[64]{0:T(128)S(1)}, s32[64]{0:T(128)}, u32[]{:S(2)}) copy-start(s32[64]{0:T(128)} %param.10) | copy-start | bytes 772
  8.6 39.0 %all-to-all-start.1 = ((f32[16,16,16,128]{3,2,1,0:T(8,128)}), f32[16,16,16,128]{3,2,1,0:T(8,128)S(1)}, u32[]{:S(2)}, u32[]{:S(2)}) async-start(f32[16,16,16,128]{3,2,1,0:T(8,128)} %get-tuple-element.32), calls=%async_computation.1 | async-start | bytes 4194304 | tf_op jit(solution)/shard_map/all_to_all | solution.py:472
  17.5 9.1 %collective-permute-start = (f32[520,128]{1,0:T(8,128)}, f32[520,128]{1,0:T(8,128)S(1)}, u32[]{:S(2)}, u32[]{:S(2)}) collective-permute-start(f32[520,128]{1,0:T(8,128)} %get-tuple-element.25), channel_id=1, source_target_pairs={{0,16},{16,32},{32,48},{48,64},{64,80},{80,96},{96,112},{112,0},{1... | collective-permute-start | bytes 798728 | tf_op jit(solution)/shard_map/ppermute | solution.py:467
  17.5 12.3 %collective-permute-start.1 = (f32[520,128]{1,0:T(8,128)}, f32[520,128]{1,0:T(8,128)S(1)}, u32[]{:S(2)}, u32[]{:S(2)}) collective-permute-start(f32[520,128]{1,0:T(8,128)} %get-tuple-element.26), channel_id=1, source_target_pairs={{0,32},{16,48},{32,64},{48,80},{64,96},{80,112},{96,0},{112,16},{1... | collective-permute-start | bytes 798728 | tf_op jit(solution)/shard_map/ppermute | solution.py:467
  19.5 21.2 %collective-permute-start.2 = (f32[520,128]{1,0:T(8,128)}, f32[520,128]{1,0:T(8,128)S(1)}, u32[]{:S(2)}, u32[]{:S(2)}) collective-permute-start(f32[520,128]{1,0:T(8,128)} %get-tuple-element.27), channel_id=1, source_target_pairs={{0,48},{16,64},{32,80},{48,96},{64,112},{80,0},{96,16},{112,32},{1... | collective-permute-start | bytes 798728 | tf_op jit(solution)/shard_map/ppermute | solution.py:467
  22.4 19.5 %collective-permute-start.3 = (f32[520,128]{1,0:T(8,128)}, f32[520,128]{1,0:T(8,128)S(1)}, u32[]{:S(2)}, u32[]{:S(2)}) collective-permute-start(f32[520,128]{1,0:T(8,128)} %get-tuple-element.28), channel_id=1, source_target_pairs={{0,64},{16,80},{32,96},{48,112},{64,0},{80,16},{96,32},{112,48},{1... | collective-permute-start | bytes 798728 | tf_op jit(solution)/shard_map/ppermute | solution.py:467
  23.6 19.6 %collective-permute-start.4 = (f32[520,128]{1,0:T(8,128)}, f32[520,128]{1,0:T(8,128)S(1)}, u32[]{:S(2)}, u32[]{:S(2)}) collective-permute-start(f32[520,128]{1,0:T(8,128)} %get-tuple-element.29), channel_id=1, source_target_pairs={{0,80},{16,96},{32,112},{48,0},{64,16},{80,32},{96,48},{112,64},{1... | collective-permute-start | bytes 798728 | tf_op jit(solution)/shard_map/ppermute | solution.py:467
  26.6 17.2 %collective-permute-start.5 = (f32[520,128]{1,0:T(8,128)}, f32[520,128]{1,0:T(8,128)S(1)}, u32[]{:S(2)}, u32[]{:S(2)}) collective-permute-start(f32[520,128]{1,0:T(8,128)} %get-tuple-element.30), channel_id=1, source_target_pairs={{0,96},{16,112},{32,0},{48,16},{64,32},{80,48},{96,64},{112,80},{1... | collective-permute-start | bytes 798728 | tf_op jit(solution)/shard_map/ppermute | solution.py:467
  29.9 15.9 %collective-permute-start.6 = (f32[520,128]{1,0:T(8,128)}, f32[520,128]{1,0:T(8,128)S(1)}, u32[]{:S(2)}, u32[]{:S(2)}) collective-permute-start(f32[520,128]{1,0:T(8,128)} %get-tuple-element.31), channel_id=1, source_target_pairs={{0,112},{16,0},{32,16},{48,32},{64,48},{80,64},{96,80},{112,96},{1... | collective-permute-start | bytes 798728 | tf_op jit(solution)/shard_map/ppermute | solution.py:467
  47.6 17.3 %all-to-all-start = ((f32[16,72,128]{2,1,0:T(8,128)}), f32[16,72,128]{2,1,0:T(8,128)S(1)}, u32[]{:S(2)}, u32[]{:S(2)}) async-start(f32[16,72,128]{2,1,0:T(8,128)} %first_modes.1), calls=%async_computation | async-start | bytes 1179648 | tf_op jit(solution)/shard_map/all_to_all | solution.py:495
  53.1 8.5 %collective-permute-start.7 = (f32[8,16,128]{2,1,0:T(8,128)}, f32[8,16,128]{2,1,0:T(8,128)S(1)}, u32[]{:S(2)}, u32[]{:S(2)}) collective-permute-start(f32[8,16,128]{2,1,0:T(8,128)} %get-tuple-element.34), channel_id=1, source_target_pairs={{0,16},{16,32},{32,48},{48,64},{64,80},{80,96},{96,112},{112,0},{1... | collective-permute-start | bytes 196616 | tf_op jit(solution)/shard_map/ppermute | solution.py:467
  53.6 9.0 %collective-permute-start.8 = (f32[8,16,128]{2,1,0:T(8,128)}, f32[8,16,128]{2,1,0:T(8,128)S(1)}, u32[]{:S(2)}, u32[]{:S(2)}) collective-permute-start(f32[8,16,128]{2,1,0:T(8,128)} %get-tuple-element.35), channel_id=1, source_target_pairs={{0,32},{16,48},{32,64},{48,80},{64,96},{80,112},{96,0},{112,16},{1... | collective-permute-start | bytes 196616 | tf_op jit(solution)/shard_map/ppermute | solution.py:467
  55.5 9.4 %collective-permute-start.9 = (f32[8,16,128]{2,1,0:T(8,128)}, f32[8,16,128]{2,1,0:T(8,128)S(1)}, u32[]{:S(2)}, u32[]{:S(2)}) collective-permute-start(f32[8,16,128]{2,1,0:T(8,128)} %get-tuple-element.36), channel_id=1, source_target_pairs={{0,48},{16,64},{32,80},{48,96},{64,112},{80,0},{96,16},{112,32},{1... | collective-permute-start | bytes 196616 | tf_op jit(solution)/shard_map/ppermute | solution.py:467
  58.0 6.9 %collective-permute-start.10 = (f32[8,16,128]{2,1,0:T(8,128)}, f32[8,16,128]{2,1,0:T(8,128)S(1)}, u32[]{:S(2)}, u32[]{:S(2)}) collective-permute-start(f32[8,16,128]{2,1,0:T(8,128)} %get-tuple-element.37), channel_id=1, source_target_pairs={{0,64},{16,80},{32,96},{48,112},{64,0},{80,16},{96,32},{112,48},{1... | collective-permute-start | bytes 196616 | tf_op jit(solution)/shard_map/ppermute | solution.py:467
  59.1 5.8 %collective-permute-start.11 = (f32[8,16,128]{2,1,0:T(8,128)}, f32[8,16,128]{2,1,0:T(8,128)S(1)}, u32[]{:S(2)}, u32[]{:S(2)}) collective-permute-start(f32[8,16,128]{2,1,0:T(8,128)} %get-tuple-element.38), channel_id=1, source_target_pairs={{0,80},{16,96},{32,112},{48,0},{64,16},{80,32},{96,48},{112,64},{1... | collective-permute-start | bytes 196616 | tf_op jit(solution)/shard_map/ppermute | solution.py:467
  61.6 4.5 %collective-permute-start.12 = (f32[8,16,128]{2,1,0:T(8,128)}, f32[8,16,128]{2,1,0:T(8,128)S(1)}, u32[]{:S(2)}, u32[]{:S(2)}) collective-permute-start(f32[8,16,128]{2,1,0:T(8,128)} %get-tuple-element.39), channel_id=1, source_target_pairs={{0,96},{16,112},{32,0},{48,16},{64,32},{80,48},{96,64},{112,80},{1... | collective-permute-start | bytes 196616 | tf_op jit(solution)/shard_map/ppermute | solution.py:467
  62.6 3.5 %collective-permute-start.13 = (f32[8,16,128]{2,1,0:T(8,128)}, f32[8,16,128]{2,1,0:T(8,128)S(1)}, u32[]{:S(2)}, u32[]{:S(2)}) collective-permute-start(f32[8,16,128]{2,1,0:T(8,128)} %get-tuple-element.40), channel_id=1, source_target_pairs={{0,112},{16,0},{32,16},{48,32},{64,48},{80,64},{96,80},{112,96},{1... | collective-permute-start | bytes 196616 | tf_op jit(solution)/shard_map/ppermute | solution.py:467

commit v3 on v2

--- a/solution.py
+++ b/solution.py
@@ -280,6 +280,25 @@
         compiler_params=pltpu.CompilerParams(vmem_limit_bytes=16 << 20),
         name="second_modes",
     )(place, tables, cross)
+
+
+def pack(gram):
+    group = lax.broadcasted_iota(jnp.int32, (8, 128), 1) // 32
+    corner = jnp.zeros((8, 128), f32)
+    for i in range(4):
+        rows = gram[32 + 8 * i : 40 + 8 * i]
+        corner = jnp.where(group == i, pltpu.roll(rows, (32 * i - 32) % 128, 1), corner)
+    upper = jnp.where(half_lanes((16, 128)), gram[:16], pltpu.roll(gram[16:32], 64, 1))
+    return jnp.concatenate([upper, corner])
+
+
+def unpack(packed):
+    upper, corner = packed[:16], packed[16:]
+    lower = jnp.concatenate([pltpu.roll(corner, (32 - 32 * i) % 128, 1) for i in range(4)])
+    half = jnp.concatenate([upper[:, :64], pltpu.roll(upper, 64, 1)[:, :64], lower[:, :64]])
+    row = lax.broadcasted_iota(jnp.int32, (M, M), 0)
+    column = lax.broadcasted_iota(jnp.int32, (M, M), 1)
+    return jnp.where((row >= 32) & (column < 32), half.T, half)
 
 
 def gram_kernel(place, first_table, table_ref, odd_weight, even_ref, *refs):
@@ -322,7 +341,7 @@
     weights = [[odd_weight[b : b + 1, :64] for b in range(b2, 8, 2)] for b2 in range(2)]
     total += add(jnp.concatenate(rows), *weights)
     gram = total[:64] + pltpu.roll(total[64:], 64, 1)
-    packed = jnp.where(half_lanes((32, 128)), gram[:32], pltpu.roll(gram[32:], 64, 1))
+    packed = pack(gram)
     for i in range(GX):
         out[i] = packed
 
@@ -332,7 +351,7 @@
         gram_kernel,
         in_specs=[SCALAR] + [WHOLE] * (GX + 4),
         out_specs=WHOLE,
-        out_shape=jax.ShapeDtypeStruct((GX, 32, 128), f32),
+        out_shape=jax.ShapeDtypeStruct((GX, 24, 128), f32),
         compiler_params=pltpu.CompilerParams(vmem_limit_bytes=16 << 20),
         name="gram",
     )(place, first_table, second_table, odd_weight, even, *odd)
@@ -352,7 +371,7 @@
     row = lax.broadcasted_iota(jnp.int32, (M, M), 0)
     column = lax.broadcasted_iota(jnp.int32, (M, M), 1)
     identity = (row == column).astype(f32)
-    matrix = identity + jnp.concatenate([packed[:, :64], packed[:, 64:]])
+    matrix = identity + unpack(packed)
     squares = jnp.sum(jnp.sum(matrix * matrix, axis=1, keepdims=True), axis=0, keepdims=True)
     frobenius = jnp.sqrt(squares)
 
@@ -496,7 +515,7 @@
     odd = [odd[0]] + [shifted(odd[s], s) for s in range(1, GX)]
     parts = gram(place, first_table, y_table, odd_weight, even, odd)
     parts = backwards(parts, "gx")
-    parts = jnp.broadcast_to(jnp.sum(parts, axis=0), (GY, 32, 128))
+    parts = jnp.broadcast_to(jnp.sum(parts, axis=0), (GY, 24, 128))
     parts = backwards(parts, "gy")
     return analyse(parts, member_order.reshape(1, M), ensemble)
 

time: 102 us -> 102 us (level)
  no operation moved by 1% of the time
where the time goes in v3:
time: 102 us
  starting transfers between devices  39.7 us (39%)
  Pallas kernels  26.2 us (26%)
  blocking collectives  21.9 us (21%)
  waiting for transfers between devices  13.6 us (13%)
    ppermute x14, starting transfers between devices, shifted(): return lax.ppermute(block, 'gx', [(i, (i + shift) % GX) for i in range(GX)])  26.7 us
    all_to_all x2, blocking collectives, backwards(): lax.all_to_all(blocks, axis, split_axis=0, concat_axis=0, tiled=True, axi...  21.9 us
    pallas_call x1, Pallas kernels, analyse(): pl.pallas_call(analysis_kernel, in_specs=[pl.BlockSpec(memory_space=pltpu...  12.5 us
    ppermute x14, waiting for transfers between devices, shifted(): return lax.ppermute(block, 'gx', [(i, (i + shift) % GX) for i in range(GX)])  11.3 us
    all_to_all x1, starting transfers between devices, backwards(): lax.all_to_all(blocks, axis, split_axis=0, concat_axis=0, tiled=True, axi...  8.9 us
    pallas_call x1, Pallas kernels, depth_modes(): pl.pallas_call(depth_kernel, grid_spec=grid_spec, out_shape=[pltpu.HBM((G...  8.61 us
    all_to_all x1, starting transfers between devices, on_device(): even = lax.all_to_all(even, 'gy', split_axis=0, concat_axis=0, tiled=True)  4.13 us
    all_to_all x1, waiting for transfers between devices, on_device(): even = lax.all_to_all(even, 'gy', split_axis=0, concat_axis=0, tiled=True)  2.29 us
  transfers between devices with their start and end apart: 16, of which 8 were waited for; matrix products, arithmetic and copies ran while one was open for 0% of the time, Pallas kernels for 4%

profile of v3, /device:TPU:0, one launch (start us, length us, event | category | flops | bytes accessed | tf_op | source)
XLA Modules:
  0.0 101.5 jit_solution(1028863701318950367)
XLA Ops:
  0.0 8.6 %depth_modes.1 = (f32[16,16,16,128]{3,2,1,0:T(8,128)}, f32[8,128]{1,0:T(8,128)S(1)}, f32[520,128]{1,0:T(8,128)S(1)}, f32[520,128]{1,0:T(8,128)}, f32[520,128]{1,...) custom-call(s32[1]{0:T(128)} %bitcast.place, ...), custom_call_target="tpu_custom_call" | custom-call | tf_op jit(solution)/shard_map/depth_modes/pallas_call | solution.py:190
  8.6 8.9 %all-to-all-start.1 = ((f32[16,16,16,128]{3,2,1,0:T(8,128)}), f32[16,16,16,128]{3,2,1,0:T(8,128)S(1)}, u32[]{:S(2)}, u32[]{:S(2)}) async-start(f32[16,16,16,128]{3,2,1,0:T(8,128)} %get-tuple-element.32), calls=%async_computation.1 | async-start | bytes 4194304 | tf_op jit(solution)/shard_map/all_to_all | solution.py:491
  17.5 0.0 collective-permute-start
  17.5 2.0 %collective-permute-start.1 = (f32[520,128]{1,0:T(8,128)}, f32[520,128]{1,0:T(8,128)S(1)}, u32[]{:S(2)}, u32[]{:S(2)}) collective-permute-start(f32[520,128]{1,0:T(8,128)} %get-tuple-element.26), channel_id=1, source_target_pairs={{0,32},{16,48},{32,64},{48,80},{64,96},{80,112},{96,0},{112,16},{1... | collective-permute-start | bytes 798728 | tf_op jit(solution)/shard_map/ppermute | solution.py:486
  19.5 2.9 %collective-permute-start.2 = (f32[520,128]{1,0:T(8,128)}, f32[520,128]{1,0:T(8,128)S(1)}, u32[]{:S(2)}, u32[]{:S(2)}) collective-permute-start(f32[520,128]{1,0:T(8,128)} %get-tuple-element.27), channel_id=1, source_target_pairs={{0,48},{16,64},{32,80},{48,96},{64,112},{80,0},{96,16},{112,32},{1... | collective-permute-start | bytes 798728 | tf_op jit(solution)/shard_map/ppermute | solution.py:486
  22.4 1.2 %collective-permute-start.3 = (f32[520,128]{1,0:T(8,128)}, f32[520,128]{1,0:T(8,128)S(1)}, u32[]{:S(2)}, u32[]{:S(2)}) collective-permute-start(f32[520,128]{1,0:T(8,128)} %get-tuple-element.28), channel_id=1, source_target_pairs={{0,64},{16,80},{32,96},{48,112},{64,0},{80,16},{96,32},{112,48},{1... | collective-permute-start | bytes 798728 | tf_op jit(solution)/shard_map/ppermute | solution.py:486
  23.6 2.5 %collective-permute-start.4 = (f32[520,128]{1,0:T(8,128)}, f32[520,128]{1,0:T(8,128)S(1)}, u32[]{:S(2)}, u32[]{:S(2)}) collective-permute-start(f32[520,128]{1,0:T(8,128)} %get-tuple-element.29), channel_id=1, source_target_pairs={{0,80},{16,96},{32,112},{48,0},{64,16},{80,32},{96,48},{112,64},{1... | collective-permute-start | bytes 798728 | tf_op jit(solution)/shard_map/ppermute | solution.py:486
  26.1 0.6 collective-permute-done.refs_1_
  26.6 3.2 %collective-permute-start.5 = (f32[520,128]{1,0:T(8,128)}, f32[520,128]{1,0:T(8,128)S(1)}, u32[]{:S(2)}, u32[]{:S(2)}) collective-permute-start(f32[520,128]{1,0:T(8,128)} %get-tuple-element.30), channel_id=1, source_target_pairs={{0,96},{16,112},{32,0},{48,16},{64,32},{80,48},{96,64},{112,80},{1... | collective-permute-start | bytes 798728 | tf_op jit(solution)/shard_map/ppermute | solution.py:486
  29.9 0.0 collective-permute-done.1.refs_2_
  29.9 5.4 %collective-permute-start.6 = (f32[520,128]{1,0:T(8,128)}, f32[520,128]{1,0:T(8,128)S(1)}, u32[]{:S(2)}, u32[]{:S(2)}) collective-permute-start(f32[520,128]{1,0:T(8,128)} %get-tuple-element.31), channel_id=1, source_target_pairs={{0,112},{16,0},{32,16},{48,32},{64,48},{80,64},{96,80},{112,96},{1... | collective-permute-start | bytes 798728 | tf_op jit(solution)/shard_map/ppermute | solution.py:486
  35.3 5.4 %collective-permute-done.2.refs_3_ = f32[520,128]{1,0:T(8,128)S(1)} collective-permute-done((f32[520,128]{1,0:T(8,128)}, f32[520,128]{1,0:T(8,128)S(1)}, u32[]{:S(2)}, u32[]{:S(2)}) %collective-permute-start.2) | collective-permute-done | bytes 266272 | tf_op jit(solution)/shard_map/ppermute | solution.py:486
  40.7 1.0 first_half.1.half
  41.7 0.2 collective-permute-done.3.refs_4_
  41.9 1.2 %collective-permute-done.4.refs_5_ = f32[520,128]{1,0:T(8,128)S(1)} collective-permute-done((f32[520,128]{1,0:T(8,128)}, f32[520,128]{1,0:T(8,128)S(1)}, u32[]{:S(2)}, u32[]{:S(2)}) %collective-permute-start.4) | collective-permute-done | bytes 266272 | tf_op jit(solution)/shard_map/ppermute | solution.py:486
  43.1 0.7 collective-permute-done.5.refs_6_
  43.9 1.9 %collective-permute-done.6.refs_7_ = f32[520,128]{1,0:T(8,128)S(1)} collective-permute-done((f32[520,128]{1,0:T(8,128)}, f32[520,128]{1,0:T(8,128)S(1)}, u32[]{:S(2)}, u32[]{:S(2)}) %collective-permute-start.6) | collective-permute-done | bytes 266272 | tf_op jit(solution)/shard_map/ppermute | solution.py:486
  45.8 1.8 %first_modes.1 = f32[16,72,128]{2,1,0:T(8,128)} custom-call(s32[1]{0:T(128)} %bitcast.place, bf16[8,128,256]{2,1,0:T(8,128)(2,1)S(1)} %copy-done, f32[8,64,256]{2,1,0:T(8,128)S(1)} %first_half.1.half, f32[520,128]{1,0:T(8,128)S(1)} %get-tuple-element.24.refs_0_, f32[520,128]{1,0:T(8,128)S(1)} %collective-permute-done.refs_1_, ...), custom_call_target="tpu_custom_call" | custom-call | tf_op jit(solution)/shard_map/first_modes/pallas_call | solution.py:244
  47.6 4.1 %all-to-all-start = ((f32[16,72,128]{2,1,0:T(8,128)}), f32[16,72,128]{2,1,0:T(8,128)S(1)}, u32[]{:S(2)}, u32[]{:S(2)}) async-start(f32[16,72,128]{2,1,0:T(8,128)} %first_modes.1), calls=%async_computation | async-start | bytes 1179648 | tf_op jit(solution)/shard_map/all_to_all | solution.py:514
  51.8 1.3 %second_modes.1 = (f32[8,16,128]{2,1,0:T(8,128)S(1)}, f32[8,16,128]{2,1,0:T(8,128)}, f32[8,16,128]{2,1,0:T(8,128)}, f32[8,16,128]{2,1,0:T(8,128)}, f32[8,16,128]...) custom-call(s32[1]{0:T(128)} %bitcast.place, f32[2,128,256]{2,1,0:T(8,128)S(1)} %copy-done.1, ...), custom_call_target="tpu_custom_call" | custom-call | tf_op jit(solution)/shard_map/second_modes/pallas_call | solution.py:274
  53.1 0.5 collective-permute-start.7
  53.6 1.9 %collective-permute-start.8 = (f32[8,16,128]{2,1,0:T(8,128)}, f32[8,16,128]{2,1,0:T(8,128)S(1)}, u32[]{:S(2)}, u32[]{:S(2)}) collective-permute-start(f32[8,16,128]{2,1,0:T(8,128)} %get-tuple-element.35), channel_id=1, source_target_pairs={{0,32},{16,48},{32,64},{48,80},{64,96},{80,112},{96,0},{112,16},{1... | collective-permute-start | bytes 196616 | tf_op jit(solution)/shard_map/ppermute | solution.py:486
  55.5 2.4 %collective-permute-start.9 = (f32[8,16,128]{2,1,0:T(8,128)}, f32[8,16,128]{2,1,0:T(8,128)S(1)}, u32[]{:S(2)}, u32[]{:S(2)}) collective-permute-start(f32[8,16,128]{2,1,0:T(8,128)} %get-tuple-element.36), channel_id=1, source_target_pairs={{0,48},{16,64},{32,80},{48,96},{64,112},{80,0},{96,16},{112,32},{1... | collective-permute-start | bytes 196616 | tf_op jit(solution)/shard_map/ppermute | solution.py:486
  58.0 1.2 %collective-permute-start.10 = (f32[8,16,128]{2,1,0:T(8,128)}, f32[8,16,128]{2,1,0:T(8,128)S(1)}, u32[]{:S(2)}, u32[]{:S(2)}) collective-permute-start(f32[8,16,128]{2,1,0:T(8,128)} %get-tuple-element.37), channel_id=1, source_target_pairs={{0,64},{16,80},{32,96},{48,112},{64,0},{80,16},{96,32},{112,48},{1... | collective-permute-start | bytes 196616 | tf_op jit(solution)/shard_map/ppermute | solution.py:486
  59.1 2.4 %collective-permute-start.11 = (f32[8,16,128]{2,1,0:T(8,128)}, f32[8,16,128]{2,1,0:T(8,128)S(1)}, u32[]{:S(2)}, u32[]{:S(2)}) collective-permute-start(f32[8,16,128]{2,1,0:T(8,128)} %get-tuple-element.38), channel_id=1, source_target_pairs={{0,80},{16,96},{32,112},{48,0},{64,16},{80,32},{96,48},{112,64},{1... | collective-permute-start | bytes 196616 | tf_op jit(solution)/shard_map/ppermute | solution.py:486
  61.6 1.0 collective-permute-start.12
  62.6 2.3 %all-to-all-done.even_ref = f32[16,72,128]{2,1,0:T(8,128)S(1)} async-done(((f32[16,72,128]{2,1,0:T(8,128)}), f32[16,72,128]{2,1,0:T(8,128)S(1)}, u32[]{:S(2)}, u32[]{:S(2)}) %all-to-all-start) | async-done | bytes 589856 | tf_op jit(solution)/shard_map/all_to_all | solution.py:514
  64.9 1.2 %collective-permute-done.12.refs_6_ = f32[8,16,128]{2,1,0:T(8,128)S(1)} collective-permute-done((f32[8,16,128]{2,1,0:T(8,128)}, f32[8,16,128]{2,1,0:T(8,128)S(1)}, u32[]{:S(2)}, u32[]{:S(2)}) %collective-permute-start.12) | collective-permute-done | bytes 65568 | tf_op jit(solution)/shard_map/ppermute | solution.py:486
  66.1 1.0 gram.1
  67.1 8.8 %all_to_all.20 = f32[8,24,128]{2,1,0:T(8,128)S(1)} all-to-all(f32[8,24,128]{2,1,0:T(8,128)S(1)} %gram.1), channel_id=1, replica_groups={{112,96,80,64,48,32,16,0},{113,97,81,65,49,33,17,1},{114,98,82,66,50,34..., dimensions={0} | all-to-all | bytes 196608 | tf_op jit(solution)/shard_map/all_to_all | solution.py:491
  75.9 13.2 %all_to_all.21.parts = f32[16,24,128]{2,1,0:T(8,128)S(1)} all-to-all(f32[16,24,128]{2,1,0:T(8,128)S(1)} %broadcast_in_dim.3), channel_id=1, replica_groups={{15,14,13,12,11,10,9,8,7,6,5,4,3,2,1,0},{31,30,29,28,27,26,25,24,23,22,..., dimensions={0} | all-to-all | bytes 393216 | tf_op jit(solution)/shard_map/all_to_all | solution.py:491
  89.1 12.5 %analysis.1 = f32[64,32,1024]{2,1,0:T(8,128)} custom-call(f32[16,24,128]{2,1,0:T(8,128)S(1)} %all_to_all.21.parts, s32[1,64]{1,0:T(1,128)S(1)} %bitcast.4, f32[64,32,1024]{2,1,0:T(8,128)} %ens_hbm.1), custom_call_target="tpu_custom_call" | custom-call | tf_op jit(solution)/shard_map/analysis/pallas_call | solution.py:463
  (16 shorter events, 0.1 us)
Async XLA Ops:
  0.0 40.7 %copy-start = (bf16[8,128,256]{2,1,0:T(8,128)(2,1)S(1)}, bf16[8,128,256]{2,1,0:T(8,128)(2,1)}, u32[]{:S(2)}) copy-start(bf16[8,128,256]{2,1,0:T(8,128)(2,1)} %constant.14.clone.table_ref.first_table) | copy-start | bytes 1572868
  0.0 51.7 %copy-start.1 = (f32[2,128,256]{2,1,0:T(8,128)S(1)}, f32[2,128,256]{2,1,0:T(8,128)}, u32[]{:S(2)}) copy-start(f32[2,128,256]{2,1,0:T(8,128)} %constant.15.clone.table_ref) | copy-start | bytes 786436
  8.6 80.4 %copy-start.2 = (s32[64]{0:T(128)S(1)}, s32[64]{0:T(128)}, u32[]{:S(2)}) copy-start(s32[64]{0:T(128)} %param.10) | copy-start | bytes 772
  8.6 39.0 %all-to-all-start.1 = ((f32[16,16,16,128]{3,2,1,0:T(8,128)}), f32[16,16,16,128]{3,2,1,0:T(8,128)S(1)}, u32[]{:S(2)}, u32[]{:S(2)}) async-start(f32[16,16,16,128]{3,2,1,0:T(8,128)} %get-tuple-element.32), calls=%async_computation.1 | async-start | bytes 4194304 | tf_op jit(solution)/shard_map/all_to_all | solution.py:491
  17.5 9.1 %collective-permute-start = (f32[520,128]{1,0:T(8,128)}, f32[520,128]{1,0:T(8,128)S(1)}, u32[]{:S(2)}, u32[]{:S(2)}) collective-permute-start(f32[520,128]{1,0:T(8,128)} %get-tuple-element.25), channel_id=1, source_target_pairs={{0,16},{16,32},{32,48},{48,64},{64,80},{80,96},{96,112},{112,0},{1... | collective-permute-start | bytes 798728 | tf_op jit(solution)/shard_map/ppermute | solution.py:486
  17.5 12.3 %collective-permute-start.1 = (f32[520,128]{1,0:T(8,128)}, f32[520,128]{1,0:T(8,128)S(1)}, u32[]{:S(2)}, u32[]{:S(2)}) collective-permute-start(f32[520,128]{1,0:T(8,128)} %get-tuple-element.26), channel_id=1, source_target_pairs={{0,32},{16,48},{32,64},{48,80},{64,96},{80,112},{96,0},{112,16},{1... | collective-permute-start | bytes 798728 | tf_op jit(solution)/shard_map/ppermute | solution.py:486
  19.5 21.2 %collective-permute-start.2 = (f32[520,128]{1,0:T(8,128)}, f32[520,128]{1,0:T(8,128)S(1)}, u32[]{:S(2)}, u32[]{:S(2)}) collective-permute-start(f32[520,128]{1,0:T(8,128)} %get-tuple-element.27), channel_id=1, source_target_pairs={{0,48},{16,64},{32,80},{48,96},{64,112},{80,0},{96,16},{112,32},{1... | collective-permute-start | bytes 798728 | tf_op jit(solution)/shard_map/ppermute | solution.py:486
  22.4 19.5 %collective-permute-start.3 = (f32[520,128]{1,0:T(8,128)}, f32[520,128]{1,0:T(8,128)S(1)}, u32[]{:S(2)}, u32[]{:S(2)}) collective-permute-start(f32[520,128]{1,0:T(8,128)} %get-tuple-element.28), channel_id=1, source_target_pairs={{0,64},{16,80},{32,96},{48,112},{64,0},{80,16},{96,32},{112,48},{1... | collective-permute-start | bytes 798728 | tf_op jit(solution)/shard_map/ppermute | solution.py:486
  23.6 19.6 %collective-permute-start.4 = (f32[520,128]{1,0:T(8,128)}, f32[520,128]{1,0:T(8,128)S(1)}, u32[]{:S(2)}, u32[]{:S(2)}) collective-permute-start(f32[520,128]{1,0:T(8,128)} %get-tuple-element.29), channel_id=1, source_target_pairs={{0,80},{16,96},{32,112},{48,0},{64,16},{80,32},{96,48},{112,64},{1... | collective-permute-start | bytes 798728 | tf_op jit(solution)/shard_map/ppermute | solution.py:486
  26.6 17.2 %collective-permute-start.5 = (f32[520,128]{1,0:T(8,128)}, f32[520,128]{1,0:T(8,128)S(1)}, u32[]{:S(2)}, u32[]{:S(2)}) collective-permute-start(f32[520,128]{1,0:T(8,128)} %get-tuple-element.30), channel_id=1, source_target_pairs={{0,96},{16,112},{32,0},{48,16},{64,32},{80,48},{96,64},{112,80},{1... | collective-permute-start | bytes 798728 | tf_op jit(solution)/shard_map/ppermute | solution.py:486
  29.9 15.9 %collective-permute-start.6 = (f32[520,128]{1,0:T(8,128)}, f32[520,128]{1,0:T(8,128)S(1)}, u32[]{:S(2)}, u32[]{:S(2)}) collective-permute-start(f32[520,128]{1,0:T(8,128)} %get-tuple-element.31), channel_id=1, source_target_pairs={{0,112},{16,0},{32,16},{48,32},{64,48},{80,64},{96,80},{112,96},{1... | collective-permute-start | bytes 798728 | tf_op jit(solution)/shard_map/ppermute | solution.py:486
  47.6 17.3 %all-to-all-start = ((f32[16,72,128]{2,1,0:T(8,128)}), f32[16,72,128]{2,1,0:T(8,128)S(1)}, u32[]{:S(2)}, u32[]{:S(2)}) async-start(f32[16,72,128]{2,1,0:T(8,128)} %first_modes.1), calls=%async_computation | async-start | bytes 1179648 | tf_op jit(solution)/shard_map/all_to_all | solution.py:514
  53.1 8.5 %collective-permute-start.7 = (f32[8,16,128]{2,1,0:T(8,128)}, f32[8,16,128]{2,1,0:T(8,128)S(1)}, u32[]{:S(2)}, u32[]{:S(2)}) collective-permute-start(f32[8,16,128]{2,1,0:T(8,128)} %get-tuple-element.34), channel_id=1, source_target_pairs={{0,16},{16,32},{32,48},{48,64},{64,80},{80,96},{96,112},{112,0},{1... | collective-permute-start | bytes 196616 | tf_op jit(solution)/shard_map/ppermute | solution.py:486
  53.6 9.0 %collective-permute-start.8 = (f32[8,16,128]{2,1,0:T(8,128)}, f32[8,16,128]{2,1,0:T(8,128)S(1)}, u32[]{:S(2)}, u32[]{:S(2)}) collective-permute-start(f32[8,16,128]{2,1,0:T(8,128)} %get-tuple-element.35), channel_id=1, source_target_pairs={{0,32},{16,48},{32,64},{48,80},{64,96},{80,112},{96,0},{112,16},{1... | collective-permute-start | bytes 196616 | tf_op jit(solution)/shard_map/ppermute | solution.py:486
  55.5 9.4 %collective-permute-start.9 = (f32[8,16,128]{2,1,0:T(8,128)}, f32[8,16,128]{2,1,0:T(8,128)S(1)}, u32[]{:S(2)}, u32[]{:S(2)}) collective-permute-start(f32[8,16,128]{2,1,0:T(8,128)} %get-tuple-element.36), channel_id=1, source_target_pairs={{0,48},{16,64},{32,80},{48,96},{64,112},{80,0},{96,16},{112,32},{1... | collective-permute-start | bytes 196616 | tf_op jit(solution)/shard_map/ppermute | solution.py:486
  58.0 6.9 %collective-permute-start.10 = (f32[8,16,128]{2,1,0:T(8,128)}, f32[8,16,128]{2,1,0:T(8,128)S(1)}, u32[]{:S(2)}, u32[]{:S(2)}) collective-permute-start(f32[8,16,128]{2,1,0:T(8,128)} %get-tuple-element.37), channel_id=1, source_target_pairs={{0,64},{16,80},{32,96},{48,112},{64,0},{80,16},{96,32},{112,48},{1... | collective-permute-start | bytes 196616 | tf_op jit(solution)/shard_map/ppermute | solution.py:486
  59.1 5.8 %collective-permute-start.11 = (f32[8,16,128]{2,1,0:T(8,128)}, f32[8,16,128]{2,1,0:T(8,128)S(1)}, u32[]{:S(2)}, u32[]{:S(2)}) collective-permute-start(f32[8,16,128]{2,1,0:T(8,128)} %get-tuple-element.38), channel_id=1, source_target_pairs={{0,80},{16,96},{32,112},{48,0},{64,16},{80,32},{96,48},{112,64},{1... | collective-permute-start | bytes 196616 | tf_op jit(solution)/shard_map/ppermute | solution.py:486
  61.6 4.5 %collective-permute-start.12 = (f32[8,16,128]{2,1,0:T(8,128)}, f32[8,16,128]{2,1,0:T(8,128)S(1)}, u32[]{:S(2)}, u32[]{:S(2)}) collective-permute-start(f32[8,16,128]{2,1,0:T(8,128)} %get-tuple-element.39), channel_id=1, source_target_pairs={{0,96},{16,112},{32,0},{48,16},{64,32},{80,48},{96,64},{112,80},{1... | collective-permute-start | bytes 196616 | tf_op jit(solution)/shard_map/ppermute | solution.py:486
  62.6 3.5 %collective-permute-start.13 = (f32[8,16,128]{2,1,0:T(8,128)}, f32[8,16,128]{2,1,0:T(8,128)S(1)}, u32[]{:S(2)}, u32[]{:S(2)}) collective-permute-start(f32[8,16,128]{2,1,0:T(8,128)} %get-tuple-element.40), channel_id=1, source_target_pairs={{0,112},{16,0},{32,16},{48,32},{64,48},{80,64},{96,80},{112,96},{1... | collective-permute-start | bytes 196616 | tf_op jit(solution)/shard_map/ppermute | solution.py:486

commit v4 on v3

--- a/solution.py
+++ b/solution.py
@@ -377,14 +377,14 @@
 
     def sweep(turn, carry):
         root, inverse = carry
-        change = 1.5 * identity - 0.5 * exact_dot(inverse, root)
+        change = 1.5 * identity + exact_dot(inverse, root)
         return exact_dot(root, change), exact_dot(change, inverse)
 
     def sweep_beside(turn, carry):
         beside(turn)
         return sweep(turn, carry)
 
-    carry = lax.fori_loop(0, 16, sweep_beside, (matrix / frobenius, identity))
+    carry = lax.fori_loop(0, 16, sweep_beside, (-0.5 * (matrix / frobenius), identity))
     _, inverse = lax.fori_loop(16, NS_ITERS, sweep, carry)
     transform = inverse / jnp.sqrt(frobenius)
     chosen = (order == row).astype(f32).T

time: 102 us -> 102 us (level)
  no operation moved by 1% of the time
where the time goes in v4:
time: 102 us; the launch traced here: 101 us
  starting transfers between devices  39.7 us (39%)
  Pallas kernels  26.1 us (26%)
  blocking collectives  21.9 us (21%)
  waiting for transfers between devices  13.6 us (13%)
    ppermute x14, starting transfers between devices, shifted(): return lax.ppermute(block, 'gx', [(i, (i + shift) % GX) for i in range(GX)])  26.7 us
    all_to_all x2, blocking collectives, backwards(): lax.all_to_all(blocks, axis, split_axis=0, concat_axis=0, tiled=True, axi...  21.9 us
    pallas_call x1, Pallas kernels, analyse(): pl.pallas_call(analysis_kernel, in_specs=[pl.BlockSpec(memory_space=pltpu...  12.4 us
    ppermute x14, waiting for transfers between devices, shifted(): return lax.ppermute(block, 'gx', [(i, (i + shift) % GX) for i in range(GX)])  11.3 us
    all_to_all x1, starting transfers between devices, backwards(): lax.all_to_all(blocks, axis, split_axis=0, concat_axis=0, tiled=True, axi...  8.9 us
    pallas_call x1, Pallas kernels, depth_modes(): pl.pallas_call(depth_kernel, grid_spec=grid_spec, out_shape=[pltpu.HBM((G...  8.61 us
    all_to_all x1, starting transfers between devices, on_device(): even = lax.all_to_all(even, 'gy', split_axis=0, concat_axis=0, tiled=True)  4.13 us
    all_to_all x1, waiting for transfers between devices, on_device(): even = lax.all_to_all(even, 'gy', split_axis=0, concat_axis=0, tiled=True)  2.29 us
  transfers between devices with their start and end apart: 16, of which 8 were waited for; matrix products, arithmetic and copies ran while one was open for 0% of the time, Pallas kernels for 4%

profile of v4, /device:TPU:0, one launch (start us, length us, event | category | flops | bytes accessed | tf_op | source)
XLA Modules:
  0.0 101.5 jit_solution(13331412849817916521)
XLA Ops:
  0.0 8.6 %depth_modes.1 = (f32[16,16,16,128]{3,2,1,0:T(8,128)}, f32[8,128]{1,0:T(8,128)S(1)}, f32[520,128]{1,0:T(8,128)S(1)}, f32[520,128]{1,0:T(8,128)}, f32[520,128]{1,...) custom-call(s32[1]{0:T(128)} %bitcast.place, ...), custom_call_target="tpu_custom_call" | custom-call | tf_op jit(solution)/shard_map/depth_modes/pallas_call | solution.py:190
  8.6 8.9 %all-to-all-start.1 = ((f32[16,16,16,128]{3,2,1,0:T(8,128)}), f32[16,16,16,128]{3,2,1,0:T(8,128)S(1)}, u32[]{:S(2)}, u32[]{:S(2)}) async-start(f32[16,16,16,128]{3,2,1,0:T(8,128)} %get-tuple-element.32), calls=%async_computation.1 | async-start | bytes 4194304 | tf_op jit(solution)/shard_map/all_to_all | solution.py:491
  17.5 0.0 collective-permute-start
  17.5 2.0 %collective-permute-start.1 = (f32[520,128]{1,0:T(8,128)}, f32[520,128]{1,0:T(8,128)S(1)}, u32[]{:S(2)}, u32[]{:S(2)}) collective-permute-start(f32[520,128]{1,0:T(8,128)} %get-tuple-element.26), channel_id=1, source_target_pairs={{0,32},{16,48},{32,64},{48,80},{64,96},{80,112},{96,0},{112,16},{1... | collective-permute-start | bytes 798728 | tf_op jit(solution)/shard_map/ppermute | solution.py:486
  19.5 2.9 %collective-permute-start.2 = (f32[520,128]{1,0:T(8,128)}, f32[520,128]{1,0:T(8,128)S(1)}, u32[]{:S(2)}, u32[]{:S(2)}) collective-permute-start(f32[520,128]{1,0:T(8,128)} %get-tuple-element.27), channel_id=1, source_target_pairs={{0,48},{16,64},{32,80},{48,96},{64,112},{80,0},{96,16},{112,32},{1... | collective-permute-start | bytes 798728 | tf_op jit(solution)/shard_map/ppermute | solution.py:486
  22.4 1.2 %collective-permute-start.3 = (f32[520,128]{1,0:T(8,128)}, f32[520,128]{1,0:T(8,128)S(1)}, u32[]{:S(2)}, u32[]{:S(2)}) collective-permute-start(f32[520,128]{1,0:T(8,128)} %get-tuple-element.28), channel_id=1, source_target_pairs={{0,64},{16,80},{32,96},{48,112},{64,0},{80,16},{96,32},{112,48},{1... | collective-permute-start | bytes 798728 | tf_op jit(solution)/shard_map/ppermute | solution.py:486
  23.6 2.5 %collective-permute-start.4 = (f32[520,128]{1,0:T(8,128)}, f32[520,128]{1,0:T(8,128)S(1)}, u32[]{:S(2)}, u32[]{:S(2)}) collective-permute-start(f32[520,128]{1,0:T(8,128)} %get-tuple-element.29), channel_id=1, source_target_pairs={{0,80},{16,96},{32,112},{48,0},{64,16},{80,32},{96,48},{112,64},{1... | collective-permute-start | bytes 798728 | tf_op jit(solution)/shard_map/ppermute | solution.py:486
  26.1 0.6 collective-permute-done.refs_1_
  26.6 3.2 %collective-permute-start.5 = (f32[520,128]{1,0:T(8,128)}, f32[520,128]{1,0:T(8,128)S(1)}, u32[]{:S(2)}, u32[]{:S(2)}) collective-permute-start(f32[520,128]{1,0:T(8,128)} %get-tuple-element.30), channel_id=1, source_target_pairs={{0,96},{16,112},{32,0},{48,16},{64,32},{80,48},{96,64},{112,80},{1... | collective-permute-start | bytes 798728 | tf_op jit(solution)/shard_map/ppermute | solution.py:486
  29.9 5.4 %collective-permute-start.6 = (f32[520,128]{1,0:T(8,128)}, f32[520,128]{1,0:T(8,128)S(1)}, u32[]{:S(2)}, u32[]{:S(2)}) collective-permute-start(f32[520,128]{1,0:T(8,128)} %get-tuple-element.31), channel_id=1, source_target_pairs={{0,112},{16,0},{32,16},{48,32},{64,48},{80,64},{96,80},{112,96},{1... | collective-permute-start | bytes 798728 | tf_op jit(solution)/shard_map/ppermute | solution.py:486
  35.3 5.4 %collective-permute-done.2.refs_3_ = f32[520,128]{1,0:T(8,128)S(1)} collective-permute-done((f32[520,128]{1,0:T(8,128)}, f32[520,128]{1,0:T(8,128)S(1)}, u32[]{:S(2)}, u32[]{:S(2)}) %collective-permute-start.2) | collective-permute-done | bytes 266272 | tf_op jit(solution)/shard_map/ppermute | solution.py:486
  40.7 1.0 first_half.1.half
  41.7 0.2 collective-permute-done.3.refs_4_
  41.9 1.2 %collective-permute-done.4.refs_5_ = f32[520,128]{1,0:T(8,128)S(1)} collective-permute-done((f32[520,128]{1,0:T(8,128)}, f32[520,128]{1,0:T(8,128)S(1)}, u32[]{:S(2)}, u32[]{:S(2)}) %collective-permute-start.4) | collective-permute-done | bytes 266272 | tf_op jit(solution)/shard_map/ppermute | solution.py:486
  43.1 0.7 collective-permute-done.5.refs_6_
  43.9 1.9 %collective-permute-done.6.refs_7_ = f32[520,128]{1,0:T(8,128)S(1)} collective-permute-done((f32[520,128]{1,0:T(8,128)}, f32[520,128]{1,0:T(8,128)S(1)}, u32[]{:S(2)}, u32[]{:S(2)}) %collective-permute-start.6) | collective-permute-done | bytes 266272 | tf_op jit(solution)/shard_map/ppermute | solution.py:486
  45.8 1.8 %first_modes.1 = f32[16,72,128]{2,1,0:T(8,128)} custom-call(s32[1]{0:T(128)} %bitcast.place, bf16[8,128,256]{2,1,0:T(8,128)(2,1)S(1)} %copy-done, f32[8,64,256]{2,1,0:T(8,128)S(1)} %first_half.1.half, f32[520,128]{1,0:T(8,128)S(1)} %get-tuple-element.24.refs_0_, f32[520,128]{1,0:T(8,128)S(1)} %collective-permute-done.refs_1_, ...), custom_call_target="tpu_custom_call" | custom-call | tf_op jit(solution)/shard_map/first_modes/pallas_call | solution.py:244
  47.6 0.0 all-to-all-done.1.cross
  47.6 4.1 %all-to-all-start = ((f32[16,72,128]{2,1,0:T(8,128)}), f32[16,72,128]{2,1,0:T(8,128)S(1)}, u32[]{:S(2)}, u32[]{:S(2)}) async-start(f32[16,72,128]{2,1,0:T(8,128)} %first_modes.1), calls=%async_computation | async-start | bytes 1179648 | tf_op jit(solution)/shard_map/all_to_all | solution.py:514
  51.8 1.3 %second_modes.1 = (f32[8,16,128]{2,1,0:T(8,128)S(1)}, f32[8,16,128]{2,1,0:T(8,128)}, f32[8,16,128]{2,1,0:T(8,128)}, f32[8,16,128]{2,1,0:T(8,128)}, f32[8,16,128]...) custom-call(s32[1]{0:T(128)} %bitcast.place, f32[2,128,256]{2,1,0:T(8,128)S(1)} %copy-done.1, ...), custom_call_target="tpu_custom_call" | custom-call | tf_op jit(solution)/shard_map/second_modes/pallas_call | solution.py:274
  53.1 0.5 collective-permute-start.7
  53.6 1.9 %collective-permute-start.8 = (f32[8,16,128]{2,1,0:T(8,128)}, f32[8,16,128]{2,1,0:T(8,128)S(1)}, u32[]{:S(2)}, u32[]{:S(2)}) collective-permute-start(f32[8,16,128]{2,1,0:T(8,128)} %get-tuple-element.35), channel_id=1, source_target_pairs={{0,32},{16,48},{32,64},{48,80},{64,96},{80,112},{96,0},{112,16},{1... | collective-permute-start | bytes 196616 | tf_op jit(solution)/shard_map/ppermute | solution.py:486
  55.5 2.4 %collective-permute-start.9 = (f32[8,16,128]{2,1,0:T(8,128)}, f32[8,16,128]{2,1,0:T(8,128)S(1)}, u32[]{:S(2)}, u32[]{:S(2)}) collective-permute-start(f32[8,16,128]{2,1,0:T(8,128)} %get-tuple-element.36), channel_id=1, source_target_pairs={{0,48},{16,64},{32,80},{48,96},{64,112},{80,0},{96,16},{112,32},{1... | collective-permute-start | bytes 196616 | tf_op jit(solution)/shard_map/ppermute | solution.py:486
  58.0 1.2 %collective-permute-start.10 = (f32[8,16,128]{2,1,0:T(8,128)}, f32[8,16,128]{2,1,0:T(8,128)S(1)}, u32[]{:S(2)}, u32[]{:S(2)}) collective-permute-start(f32[8,16,128]{2,1,0:T(8,128)} %get-tuple-element.37), channel_id=1, source_target_pairs={{0,64},{16,80},{32,96},{48,112},{64,0},{80,16},{96,32},{112,48},{1... | collective-permute-start | bytes 196616 | tf_op jit(solution)/shard_map/ppermute | solution.py:486
  59.1 2.4 %collective-permute-start.11 = (f32[8,16,128]{2,1,0:T(8,128)}, f32[8,16,128]{2,1,0:T(8,128)S(1)}, u32[]{:S(2)}, u32[]{:S(2)}) collective-permute-start(f32[8,16,128]{2,1,0:T(8,128)} %get-tuple-element.38), channel_id=1, source_target_pairs={{0,80},{16,96},{32,112},{48,0},{64,16},{80,32},{96,48},{112,64},{1... | collective-permute-start | bytes 196616 | tf_op jit(solution)/shard_map/ppermute | solution.py:486
  61.6 1.0 collective-permute-start.12
  62.6 2.3 %all-to-all-done.even_ref = f32[16,72,128]{2,1,0:T(8,128)S(1)} async-done(((f32[16,72,128]{2,1,0:T(8,128)}), f32[16,72,128]{2,1,0:T(8,128)S(1)}, u32[]{:S(2)}, u32[]{:S(2)}) %all-to-all-start) | async-done | bytes 589856 | tf_op jit(solution)/shard_map/all_to_all | solution.py:514
  64.9 1.2 %collective-permute-done.12.refs_6_ = f32[8,16,128]{2,1,0:T(8,128)S(1)} collective-permute-done((f32[8,16,128]{2,1,0:T(8,128)}, f32[8,16,128]{2,1,0:T(8,128)S(1)}, u32[]{:S(2)}, u32[]{:S(2)}) %collective-permute-start.12) | collective-permute-done | bytes 65568 | tf_op jit(solution)/shard_map/ppermute | solution.py:486
  66.1 1.0 gram.1
  67.1 8.8 %all_to_all.20 = f32[8,24,128]{2,1,0:T(8,128)S(1)} all-to-all(f32[8,24,128]{2,1,0:T(8,128)S(1)} %gram.1), channel_id=1, replica_groups={{112,96,80,64,48,32,16,0},{113,97,81,65,49,33,17,1},{114,98,82,66,50,34..., dimensions={0} | all-to-all | bytes 196608 | tf_op jit(solution)/shard_map/all_to_all | solution.py:491
  75.9 13.2 %all_to_all.21.parts = f32[16,24,128]{2,1,0:T(8,128)S(1)} all-to-all(f32[16,24,128]{2,1,0:T(8,128)S(1)} %broadcast_in_dim.3), channel_id=1, replica_groups={{15,14,13,12,11,10,9,8,7,6,5,4,3,2,1,0},{31,30,29,28,27,26,25,24,23,22,..., dimensions={0} | all-to-all | bytes 393216 | tf_op jit(solution)/shard_map/all_to_all | solution.py:491
  89.1 12.4 %analysis.1 = f32[64,32,1024]{2,1,0:T(8,128)} custom-call(f32[16,24,128]{2,1,0:T(8,128)S(1)} %all_to_all.21.parts, s32[1,64]{1,0:T(1,128)S(1)} %bitcast.4, f32[64,32,1024]{2,1,0:T(8,128)} %ens_hbm.1), custom_call_target="tpu_custom_call" | custom-call | tf_op jit(solution)/shard_map/analysis/pallas_call | solution.py:463
  (16 shorter events, 0.1 us)
Async XLA Ops:
  0.0 40.7 %copy-start = (bf16[8,128,256]{2,1,0:T(8,128)(2,1)S(1)}, bf16[8,128,256]{2,1,0:T(8,128)(2,1)}, u32[]{:S(2)}) copy-start(bf16[8,128,256]{2,1,0:T(8,128)(2,1)} %constant.14.clone.table_ref.first_table) | copy-start | bytes 1572868
  0.0 51.7 %copy-start.1 = (f32[2,128,256]{2,1,0:T(8,128)S(1)}, f32[2,128,256]{2,1,0:T(8,128)}, u32[]{:S(2)}) copy-start(f32[2,128,256]{2,1,0:T(8,128)} %constant.15.clone.table_ref) | copy-start | bytes 786436
  8.6 80.4 %copy-start.2 = (s32[64]{0:T(128)S(1)}, s32[64]{0:T(128)}, u32[]{:S(2)}) copy-start(s32[64]{0:T(128)} %param.10) | copy-start | bytes 772
  8.6 39.0 %all-to-all-start.1 = ((f32[16,16,16,128]{3,2,1,0:T(8,128)}), f32[16,16,16,128]{3,2,1,0:T(8,128)S(1)}, u32[]{:S(2)}, u32[]{:S(2)}) async-start(f32[16,16,16,128]{3,2,1,0:T(8,128)} %get-tuple-element.32), calls=%async_computation.1 | async-start | bytes 4194304 | tf_op jit(solution)/shard_map/all_to_all | solution.py:491
  17.5 9.1 %collective-permute-start = (f32[520,128]{1,0:T(8,128)}, f32[520,128]{1,0:T(8,128)S(1)}, u32[]{:S(2)}, u32[]{:S(2)}) collective-permute-start(f32[520,128]{1,0:T(8,128)} %get-tuple-element.25), channel_id=1, source_target_pairs={{0,16},{16,32},{32,48},{48,64},{64,80},{80,96},{96,112},{112,0},{1... | collective-permute-start | bytes 798728 | tf_op jit(solution)/shard_map/ppermute | solution.py:486
  17.5 12.3 %collective-permute-start.1 = (f32[520,128]{1,0:T(8,128)}, f32[520,128]{1,0:T(8,128)S(1)}, u32[]{:S(2)}, u32[]{:S(2)}) collective-permute-start(f32[520,128]{1,0:T(8,128)} %get-tuple-element.26), channel_id=1, source_target_pairs={{0,32},{16,48},{32,64},{48,80},{64,96},{80,112},{96,0},{112,16},{1... | collective-permute-start | bytes 798728 | tf_op jit(solution)/shard_map/ppermute | solution.py:486
  19.5 21.2 %collective-permute-start.2 = (f32[520,128]{1,0:T(8,128)}, f32[520,128]{1,0:T(8,128)S(1)}, u32[]{:S(2)}, u32[]{:S(2)}) collective-permute-start(f32[520,128]{1,0:T(8,128)} %get-tuple-element.27), channel_id=1, source_target_pairs={{0,48},{16,64},{32,80},{48,96},{64,112},{80,0},{96,16},{112,32},{1... | collective-permute-start | bytes 798728 | tf_op jit(solution)/shard_map/ppermute | solution.py:486
  22.4 19.5 %collective-permute-start.3 = (f32[520,128]{1,0:T(8,128)}, f32[520,128]{1,0:T(8,128)S(1)}, u32[]{:S(2)}, u32[]{:S(2)}) collective-permute-start(f32[520,128]{1,0:T(8,128)} %get-tuple-element.28), channel_id=1, source_target_pairs={{0,64},{16,80},{32,96},{48,112},{64,0},{80,16},{96,32},{112,48},{1... | collective-permute-start | bytes 798728 | tf_op jit(solution)/shard_map/ppermute | solution.py:486
  23.6 19.6 %collective-permute-start.4 = (f32[520,128]{1,0:T(8,128)}, f32[520,128]{1,0:T(8,128)S(1)}, u32[]{:S(2)}, u32[]{:S(2)}) collective-permute-start(f32[520,128]{1,0:T(8,128)} %get-tuple-element.29), channel_id=1, source_target_pairs={{0,80},{16,96},{32,112},{48,0},{64,16},{80,32},{96,48},{112,64},{1... | collective-permute-start | bytes 798728 | tf_op jit(solution)/shard_map/ppermute | solution.py:486
  26.6 17.2 %collective-permute-start.5 = (f32[520,128]{1,0:T(8,128)}, f32[520,128]{1,0:T(8,128)S(1)}, u32[]{:S(2)}, u32[]{:S(2)}) collective-permute-start(f32[520,128]{1,0:T(8,128)} %get-tuple-element.30), channel_id=1, source_target_pairs={{0,96},{16,112},{32,0},{48,16},{64,32},{80,48},{96,64},{112,80},{1... | collective-permute-start | bytes 798728 | tf_op jit(solution)/shard_map/ppermute | solution.py:486
  29.9 15.9 %collective-permute-start.6 = (f32[520,128]{1,0:T(8,128)}, f32[520,128]{1,0:T(8,128)S(1)}, u32[]{:S(2)}, u32[]{:S(2)}) collective-permute-start(f32[520,128]{1,0:T(8,128)} %get-tuple-element.31), channel_id=1, source_target_pairs={{0,112},{16,0},{32,16},{48,32},{64,48},{80,64},{96,80},{112,96},{1... | collective-permute-start | bytes 798728 | tf_op jit(solution)/shard_map/ppermute | solution.py:486
  47.6 17.3 %all-to-all-start = ((f32[16,72,128]{2,1,0:T(8,128)}), f32[16,72,128]{2,1,0:T(8,128)S(1)}, u32[]{:S(2)}, u32[]{:S(2)}) async-start(f32[16,72,128]{2,1,0:T(8,128)} %first_modes.1), calls=%async_computation | async-start | bytes 1179648 | tf_op jit(solution)/shard_map/all_to_all | solution.py:514
  53.1 8.5 %collective-permute-start.7 = (f32[8,16,128]{2,1,0:T(8,128)}, f32[8,16,128]{2,1,0:T(8,128)S(1)}, u32[]{:S(2)}, u32[]{:S(2)}) collective-permute-start(f32[8,16,128]{2,1,0:T(8,128)} %get-tuple-element.34), channel_id=1, source_target_pairs={{0,16},{16,32},{32,48},{48,64},{64,80},{80,96},{96,112},{112,0},{1... | collective-permute-start | bytes 196616 | tf_op jit(solution)/shard_map/ppermute | solution.py:486
  53.6 9.0 %collective-permute-start.8 = (f32[8,16,128]{2,1,0:T(8,128)}, f32[8,16,128]{2,1,0:T(8,128)S(1)}, u32[]{:S(2)}, u32[]{:S(2)}) collective-permute-start(f32[8,16,128]{2,1,0:T(8,128)} %get-tuple-element.35), channel_id=1, source_target_pairs={{0,32},{16,48},{32,64},{48,80},{64,96},{80,112},{96,0},{112,16},{1... | collective-permute-start | bytes 196616 | tf_op jit(solution)/shard_map/ppermute | solution.py:486
  55.5 9.4 %collective-permute-start.9 = (f32[8,16,128]{2,1,0:T(8,128)}, f32[8,16,128]{2,1,0:T(8,128)S(1)}, u32[]{:S(2)}, u32[]{:S(2)}) collective-permute-start(f32[8,16,128]{2,1,0:T(8,128)} %get-tuple-element.36), channel_id=1, source_target_pairs={{0,48},{16,64},{32,80},{48,96},{64,112},{80,0},{96,16},{112,32},{1... | collective-permute-start | bytes 196616 | tf_op jit(solution)/shard_map/ppermute | solution.py:486
  58.0 6.9 %collective-permute-start.10 = (f32[8,16,128]{2,1,0:T(8,128)}, f32[8,16,128]{2,1,0:T(8,128)S(1)}, u32[]{:S(2)}, u32[]{:S(2)}) collective-permute-start(f32[8,16,128]{2,1,0:T(8,128)} %get-tuple-element.37), channel_id=1, source_target_pairs={{0,64},{16,80},{32,96},{48,112},{64,0},{80,16},{96,32},{112,48},{1... | collective-permute-start | bytes 196616 | tf_op jit(solution)/shard_map/ppermute | solution.py:486
  59.1 5.8 %collective-permute-start.11 = (f32[8,16,128]{2,1,0:T(8,128)}, f32[8,16,128]{2,1,0:T(8,128)S(1)}, u32[]{:S(2)}, u32[]{:S(2)}) collective-permute-start(f32[8,16,128]{2,1,0:T(8,128)} %get-tuple-element.38), channel_id=1, source_target_pairs={{0,80},{16,96},{32,112},{48,0},{64,16},{80,32},{96,48},{112,64},{1... | collective-permute-start | bytes 196616 | tf_op jit(solution)/shard_map/ppermute | solution.py:486
  61.6 4.5 %collective-permute-start.12 = (f32[8,16,128]{2,1,0:T(8,128)}, f32[8,16,128]{2,1,0:T(8,128)S(1)}, u32[]{:S(2)}, u32[]{:S(2)}) collective-permute-start(f32[8,16,128]{2,1,0:T(8,128)} %get-tuple-element.39), channel_id=1, source_target_pairs={{0,96},{16,112},{32,0},{48,16},{64,32},{80,48},{96,64},{112,80},{1... | collective-permute-start | bytes 196616 | tf_op jit(solution)/shard_map/ppermute | solution.py:486
  62.6 3.5 %collective-permute-start.13 = (f32[8,16,128]{2,1,0:T(8,128)}, f32[8,16,128]{2,1,0:T(8,128)S(1)}, u32[]{:S(2)}, u32[]{:S(2)}) collective-permute-start(f32[8,16,128]{2,1,0:T(8,128)} %get-tuple-element.40), channel_id=1, source_target_pairs={{0,112},{16,0},{32,16},{48,32},{64,48},{80,64},{96,80},{112,96},{1... | collective-permute-start | bytes 196616 | tf_op jit(solution)/shard_map/ppermute | solution.py:486
